TPU v7x, 32 devices: a whole 2x2x4 slice. The times are simulated.
32 devices in a mesh: ctx: 8 (over y, x, core), tp: 4 (over z).
Axes of the slice: x: 2, y: 2, z: 4, core: 2. Of those that a mesh axis runs over, the one named last changes fastest.
Arguments:
- queries: bfloat16 [2048, 64, 128], P('ctx', 'tp'), may hold values from -24 to 24
- keys: bfloat16 [2048, 8, 128], P('ctx', 'tp'), may hold values from -24 to 24
- values: bfloat16 [2048, 8, 128], P('ctx', 'tp'), may hold values from -6 to 6
- positions: int32 [2048], replicated, may hold values from 0 to 2047, as said below
- out_weight: bfloat16 [8192, 8192], P('tp'), may hold values from -0.0625 to 0.0625
- grad_out: bfloat16 [2048, 8192], P('ctx'), may hold values from -6 to 6
Outputs:
- layer_out: bfloat16 [2048, 8192], P('ctx', 'tp')
- grad_queries: bfloat16 [2048, 64, 128], P('ctx', 'tp')
- grad_keys: bfloat16 [2048, 8, 128], P('ctx', 'tp')
- grad_values: bfloat16 [2048, 8, 128], P('ctx', 'tp')
Inputs may be any that keep to these rules, and one draw needn't show every extreme that they name: positions is a permutation of 0 to 2047. The rows of each index of ctx (256 rows) hold two whole blocks of 128 consecutive positions in rising order: block numbers b and 15 - b, in either order; which b a device holds is drawn.
All inputs are finite; a program needn't handle non-finite values.
Results may differ from a plain program's by a relative error of at most 0.035.
Values may be sent and summed in bfloat16 or wider, within the bound.
A program may use at most 128 MiB of HBM per device.

v0:
```python
import math

import jax
import jax.numpy as jnp
from jax import lax
from jax.sharding import PartitionSpec as P

NEG_FILL = -1e30


def masked_scores(qgroups, key_block, query_pos, key_pos):
    scores = jnp.einsum("rngd,knd->ngrk", qgroups, key_block, preferred_element_type=jnp.float32)
    scores = scores * (1.0 / math.sqrt(qgroups.shape[-1]))
    allowed = key_pos[None, :] <= query_pos[:, None]
    return jnp.where(allowed, scores, NEG_FILL)


def online_step(state_now, qgroups, key_block, value_block, query_pos, key_pos):
    running, row_total, accumulated = state_now
    scores = masked_scores(qgroups, key_block, query_pos, key_pos)
    new_top = jnp.maximum(running, jnp.max(scores, axis=-1))
    factor = jnp.exp(running - new_top)
    weights = jnp.exp(scores - new_top[..., None])
    row_total = row_total * factor + jnp.sum(weights, axis=-1)
    accumulated = accumulated * factor[..., None] + jnp.einsum(
        "ngrk,knd->ngrd",
        weights.astype(jnp.bfloat16),
        value_block,
        preferred_element_type=jnp.float32,
    )
    return (new_top, row_total, accumulated)


def block_grads(
    qgroups, grad_groups, log_total, row_delta, key_block, value_block, query_pos, key_pos
):
    scores = masked_scores(qgroups, key_block, query_pos, key_pos)
    weights = jnp.exp(scores - log_total[..., None])
    weights_bf = weights.astype(jnp.bfloat16)
    dweights = jnp.einsum(
        "rngd,knd->ngrk", grad_groups, value_block, preferred_element_type=jnp.float32
    )
    dscores = (weights * (dweights - row_delta[..., None])).astype(jnp.bfloat16)
    return (dscores, weights_bf)


def local(queries, keys, values, positions, out_weight, grad_out):
    local_rows = queries.shape[0]
    kv_local = keys.shape[1]
    head_dim = keys.shape[2]
    group_size = queries.shape[1] // kv_local
    ctx_count = lax.axis_size("ctx")
    seq_len = local_rows * ctx_count
    key_rows = local_rows * math.gcd(max(1, 512 // local_rows), ctx_count)
    block_count = seq_len // key_rows
    score_scale = 1.0 / math.sqrt(head_dim)
    query_pos = lax.dynamic_slice_in_dim(positions, lax.axis_index("ctx") * local_rows, local_rows)
    qgroups = queries.reshape(local_rows, kv_local, group_size, head_dim)
    start_state = (
        jnp.full((kv_local, group_size, local_rows), NEG_FILL, jnp.float32),
        jnp.zeros((kv_local, group_size, local_rows), jnp.float32),
        jnp.zeros((kv_local, group_size, local_rows, head_dim), jnp.float32),
    )
    key_all, value_all = (
        lax.all_gather(keys, "ctx", axis=0, tiled=True),
        lax.all_gather(values, "ctx", axis=0, tiled=True),
    )

    def forward_block(index_now, state_now):
        first_row = index_now * key_rows
        return online_step(
            state_now,
            qgroups,
            lax.dynamic_slice_in_dim(key_all, first_row, key_rows),
            lax.dynamic_slice_in_dim(value_all, first_row, key_rows),
            query_pos,
            lax.dynamic_slice_in_dim(positions, first_row, key_rows),
        )

    running, row_total, accumulated = lax.fori_loop(0, block_count, forward_block, start_state)
    attended = (accumulated / row_total[..., None]).astype(jnp.bfloat16)
    log_total = running + jnp.log(row_total)
    weight_grid = out_weight.reshape(kv_local, group_size, head_dim, out_weight.shape[1])
    partial_out = jnp.einsum(
        "ngrd,ngde->re", attended, weight_grid, preferred_element_type=jnp.float32
    ).astype(jnp.bfloat16)
    layer_out = (
        lax.psum_scatter(partial_out, "tp", scatter_dimension=1, tiled=True)
        .astype(jnp.float32)
        .astype(jnp.bfloat16)
    )
    grad_heads = lax.dot_general(
        grad_out, out_weight, (((1,), (1,)), ((), ())), preferred_element_type=jnp.float32
    ).astype(jnp.bfloat16)
    grad_groups = grad_heads.reshape(local_rows, kv_local, group_size, head_dim)
    row_delta = jnp.einsum(
        "ngrd,rngd->ngr", attended.astype(jnp.float32), grad_groups.astype(jnp.float32)
    )

    def grads_for(first_row, row_count):
        key_block = lax.dynamic_slice_in_dim(key_all, first_row, row_count)
        value_block = lax.dynamic_slice_in_dim(value_all, first_row, row_count)
        key_pos = lax.dynamic_slice_in_dim(positions, first_row, row_count)
        dscores, weights_bf = block_grads(
            qgroups, grad_groups, log_total, row_delta, key_block, value_block, query_pos, key_pos
        )
        return (key_block, dscores, weights_bf)

    def key_terms(dscores, weights_bf):
        grad_key = (
            jnp.einsum("ngrk,rngd->knd", dscores, qgroups, preferred_element_type=jnp.float32)
            * score_scale
        )
        grad_value = jnp.einsum(
            "ngrk,rngd->knd", weights_bf, grad_groups, preferred_element_type=jnp.float32
        )
        return jnp.stack([grad_key, grad_value], axis=1)

    def query_term(dscores, key_block):
        return jnp.einsum("ngrk,knd->rngd", dscores, key_block, preferred_element_type=jnp.float32)

    zero_query = jnp.zeros((local_rows, kv_local, group_size, head_dim), jnp.float32)

    def backward_block(grad_query, index_now):
        key_block, dscores, weights_bf = grads_for(index_now * key_rows, key_rows)
        return (grad_query + query_term(dscores, key_block), key_terms(dscores, weights_bf))

    grad_query, stacked = lax.scan(
        backward_block, zero_query, jnp.arange(block_count, dtype=jnp.int32)
    )
    key_value_terms = stacked.reshape(seq_len, 2, kv_local, head_dim)
    owned = lax.psum_scatter(
        key_value_terms.astype(jnp.bfloat16), "ctx", scatter_dimension=0, tiled=True
    ).astype(jnp.float32)
    grad_queries = (
        (grad_query * score_scale)
        .astype(jnp.bfloat16)
        .reshape(local_rows, kv_local * group_size, head_dim)
    )
    return (
        layer_out,
        grad_queries,
        owned[:, 0].astype(jnp.bfloat16),
        owned[:, 1].astype(jnp.bfloat16),
    )


def solution(mesh):
    placed = (
        P("ctx", "tp", None),
        P("ctx", "tp", None),
        P("ctx", "tp", None),
        P(),
        P("tp", None),
        P("ctx", None),
    )
    return jax.shard_map(
        local,
        mesh=mesh,
        in_specs=placed,
        out_specs=(
            P("ctx", "tp"),
            P("ctx", "tp", None),
            P("ctx", "tp", None),
            P("ctx", "tp", None),
        ),
        check_vma=False,
    )
```

profile of v0, /device:TPU:0, one launch (start us, length us, event | category | flops | bytes accessed | tf_op | source)
XLA Modules:
  0.0 298.9 jit_solution(5958512530040150970)
XLA Ops:
  12.1 16.7 %fusion.53 = bf16[32,8,16,128]{3,1,2,0:T(8,128)(2,1)} fusion(bf16[256,8192]{1,0:T(8,128)(2,1)} %param.15, bf16[2048,8192]{1,0:T(8,128)(2,1)} %param.14), kind=kOutput, calls=%fused_computation.60 | convolution fusion | flops 8590458880 | bytes 38797312 | tf_op jit(solution)/shard_map/dot_general | solution.py:92
  32.6 4.1 %all-gather.3.cloned.1.call-done = bf16[2048,2,128]{2,0,1:T(8,128)(2,1)} async-done(((bf16[256,2,128]{2,0,1:T(8,128)(2,1)}), bf16[2048,2,128]{2,0,1:T(8,128)(2,1)}) %all-gather.3.cloned.1.call-update) | async-done | bytes 1048592 | tf_op jit(solution)/shard_map/all_gather | solution.py:65
  36.7 26.0 %all-gather.5.cloned.1.call-done = bf16[2048,2,128]{2,0,1:T(8,128)(2,1)} async-done(((bf16[256,2,128]{2,0,1:T(8,128)(2,1)}), bf16[2048,2,128]{2,0,1:T(8,128)(2,1)}) %all-gather.5.cloned.1.call-update) | async-done | bytes 1048592 | tf_op jit(solution)/shard_map/all_gather | solution.py:66
  62.7 39.2 %while.31 = (s32[]{:T(128)}, f32[2,8,256]{2,1,0:T(8,128)S(1)}, f32[2,8,256]{2,1,0:T(8,128)S(1)}, f32[2,8,256,128]{3,2,1,0:T(8,128)}, s32[2048]{0:T(1024)S(1)}, /...) while((s32[]{:T(128)}, f32[2,8,256]{2,1,0:T(8,128)S(1)}, ...), condition=%wide.region_3.4_spmd.clone, body=%wide.region_0.3_spmd.clone.sunk | while | flops 1098534912 | bytes 48504064 | solution.py:80
  62.9 2.3 fusion.90
  67.1 4.1 %fusion.93 = f32[2,8,256,128]{3,2,1,0:T(8,128)S(1)} fusion(f32[2,8,256,128]{3,2,1,0:T(8,128)S(1)} %copy-done.2, f32[2,512,256,8]{2,1,3,0:T(8,128)S(1)} %get-tuple-element.492, f32[2,8,256]{2,1,0:T(8,128)S(1)} %select_maximum_fusion.2, pred[256,512]{0,1:T(8,128)(4,1)S(1)} %broadcast_compare_fusion.4, f32[2,8,256]{2,1,0:T(8,128)S(1)} %get-tuple-element.494, ...), kind=kOutput, calls=%fused_computation.8.clone.1 | convolution fusion | flops 546832384 | bytes 13008901 | tf_op jit(solution)/shard_map/while/body/eval_jaxpr/ngrk,knd->ngrd/dot_general | solution.py:25
  72.7 2.3 fusion.90
  76.9 4.1 %fusion.93 = f32[2,8,256,128]{3,2,1,0:T(8,128)S(1)} fusion(f32[2,8,256,128]{3,2,1,0:T(8,128)S(1)} %copy-done.2, f32[2,512,256,8]{2,1,3,0:T(8,128)S(1)} %get-tuple-element.492, f32[2,8,256]{2,1,0:T(8,128)S(1)} %select_maximum_fusion.2, pred[256,512]{0,1:T(8,128)(4,1)S(1)} %broadcast_compare_fusion.4, f32[2,8,256]{2,1,0:T(8,128)S(1)} %get-tuple-element.494, ...), kind=kOutput, calls=%fused_computation.8.clone.1 | convolution fusion | flops 546832384 | bytes 13008901 | tf_op jit(solution)/shard_map/while/body/eval_jaxpr/ngrk,knd->ngrd/dot_general | solution.py:25
  82.5 2.3 fusion.90
  86.7 4.1 %fusion.93 = f32[2,8,256,128]{3,2,1,0:T(8,128)S(1)} fusion(f32[2,8,256,128]{3,2,1,0:T(8,128)S(1)} %copy-done.2, f32[2,512,256,8]{2,1,3,0:T(8,128)S(1)} %get-tuple-element.492, f32[2,8,256]{2,1,0:T(8,128)S(1)} %select_maximum_fusion.2, pred[256,512]{0,1:T(8,128)(4,1)S(1)} %broadcast_compare_fusion.4, f32[2,8,256]{2,1,0:T(8,128)S(1)} %get-tuple-element.494, ...), kind=kOutput, calls=%fused_computation.8.clone.1 | convolution fusion | flops 546832384 | bytes 13008901 | tf_op jit(solution)/shard_map/while/body/eval_jaxpr/ngrk,knd->ngrd/dot_general | solution.py:25
  92.3 2.3 fusion.90
  96.5 4.1 %fusion.93 = f32[2,8,256,128]{3,2,1,0:T(8,128)S(1)} fusion(f32[2,8,256,128]{3,2,1,0:T(8,128)S(1)} %copy-done.2, f32[2,512,256,8]{2,1,3,0:T(8,128)S(1)} %get-tuple-element.492, f32[2,8,256]{2,1,0:T(8,128)S(1)} %select_maximum_fusion.2, pred[256,512]{0,1:T(8,128)(4,1)S(1)} %broadcast_compare_fusion.4, f32[2,8,256]{2,1,0:T(8,128)S(1)} %get-tuple-element.494, ...), kind=kOutput, calls=%fused_computation.8.clone.1 | convolution fusion | flops 546832384 | bytes 13008901 | tf_op jit(solution)/shard_map/while/body/eval_jaxpr/ngrk,knd->ngrd/dot_general | solution.py:25
  101.9 2.8 fusion.55
  106.3 55.8 %while.32 = (s32[]{:T(128)}, f32[256,2,8,128]{0,3,2,1:T(8,128)S(1)}, bf16[4,512,2,2,128]{4,1,3,2,0:T(8,128)(2,1)}, s32[4]{0:T(128)S(1)}, bf16[2048,2,128]{2,0,1:...) while((s32[]{:T(128)}, ...), condition=%wide.region_6.7_spmd.clone, body=%wide.region_5.6_spmd.clone.sunk | while | flops 2707816448 | bytes 53140752 | solution.py:128
  112.2 3.8 %fusion.105 = bf16[2,8,256,512]{2,3,1,0:T(8,128)(2,1)S(1)} fusion(f32[2,512,256,8]{2,1,3,0:T(8,128)S(1)} %fusion.104, f32[2,8,256]{2,1,0:T(8,128)S(1)} %get-tuple-element.589, f32[2,8,256]{2,1,0:T(8,128)S(1)} %get-tuple-element.586, pred[256,512]{0,1:T(8,128)(4,1)S(1)} %broadcast_compare_fusion.5, bf16[256,2,8,128]{3,0,2,1:T(8,128)(2,1)S(1)} %copy-done.5, ...), kind=kOutput, calls=%fused_computation.25.clone.1 | convolution fusion | flops 549453824 | bytes 14057476 | tf_op jit(solution)/shard_map/while/body/eval_jaxpr/rngd,knd->ngrk/dot_general | solution.py:40
  121.9 2.3 fusion.104
  126.1 3.8 %fusion.105 = bf16[2,8,256,512]{2,3,1,0:T(8,128)(2,1)S(1)} fusion(f32[2,512,256,8]{2,1,3,0:T(8,128)S(1)} %fusion.104, f32[2,8,256]{2,1,0:T(8,128)S(1)} %get-tuple-element.589, f32[2,8,256]{2,1,0:T(8,128)S(1)} %get-tuple-element.586, pred[256,512]{0,1:T(8,128)(4,1)S(1)} %broadcast_compare_fusion.5, bf16[256,2,8,128]{3,0,2,1:T(8,128)(2,1)S(1)} %copy-done.5, ...), kind=kOutput, calls=%fused_computation.25.clone.1 | convolution fusion | flops 549453824 | bytes 14057476 | tf_op jit(solution)/shard_map/while/body/eval_jaxpr/rngd,knd->ngrk/dot_general | solution.py:40
  140.0 3.8 %fusion.105 = bf16[2,8,256,512]{2,3,1,0:T(8,128)(2,1)S(1)} fusion(f32[2,512,256,8]{2,1,3,0:T(8,128)S(1)} %fusion.104, f32[2,8,256]{2,1,0:T(8,128)S(1)} %get-tuple-element.589, f32[2,8,256]{2,1,0:T(8,128)S(1)} %get-tuple-element.586, pred[256,512]{0,1:T(8,128)(4,1)S(1)} %broadcast_compare_fusion.5, bf16[256,2,8,128]{3,0,2,1:T(8,128)(2,1)S(1)} %copy-done.5, ...), kind=kOutput, calls=%fused_computation.25.clone.1 | convolution fusion | flops 549453824 | bytes 14057476 | tf_op jit(solution)/shard_map/while/body/eval_jaxpr/rngd,knd->ngrk/dot_general | solution.py:40
  153.9 3.8 %fusion.105 = bf16[2,8,256,512]{2,3,1,0:T(8,128)(2,1)S(1)} fusion(f32[2,512,256,8]{2,1,3,0:T(8,128)S(1)} %fusion.104, f32[2,8,256]{2,1,0:T(8,128)S(1)} %get-tuple-element.589, f32[2,8,256]{2,1,0:T(8,128)S(1)} %get-tuple-element.586, pred[256,512]{0,1:T(8,128)(4,1)S(1)} %broadcast_compare_fusion.5, bf16[256,2,8,128]{3,0,2,1:T(8,128)(2,1)S(1)} %copy-done.5, ...), kind=kOutput, calls=%fused_computation.25.clone.1 | convolution fusion | flops 549453824 | bytes 14057476 | tf_op jit(solution)/shard_map/while/body/eval_jaxpr/rngd,knd->ngrk/dot_general | solution.py:40
  162.1 5.1 %copy.52 = bf16[4,512,2,2,128]{4,3,2,1,0:T(2,128)(2,1)} copy(bf16[4,512,2,2,128]{4,1,3,2,0:T(8,128)(2,1)} %get-tuple-element.227) | data formatting | bytes 4194304 | tf_op jit(solution)/shard_map/convert_element_type | solution.py:133
  167.1 4.2 %reshape.50 = bf16[2048,512]{1,0:T(8,128)(2,1)} reshape(bf16[2048,2,2,128]{3,2,1,0:T(2,128)(2,1)} %bitcast.170) | data formatting | bytes 4194304
  171.4 17.5 %fusion.50 = bf16[256,8192]{1,0:T(8,128)(2,1)} fusion(bf16[2,8,128,8192]{3,2,1,0:T(8,128)(2,1)} %bitcast.172, bf16[2,8,256,128]{3,2,1,0:T(8,128)(2,1)S(1)} %copy-done.4), kind=kOutput, calls=%fused_computation.55 | convolution fusion | flops 8592031744 | bytes 38797312 | tf_op jit(solution)/shard_map/ngrd,ngde->re/dot_general | solution.py:84
  191.0 21.7 %reduce-scatter.8.cloned.1.call-done = bf16[256,512]{1,0:T(8,128)(2,1)} async-done(((bf16[2048,512]{1,0:T(8,128)(2,1)}), bf16[256,512]{1,0:T(8,128)(2,1)}) %reduce-scatter.8.cloned.1.call-update) | async-done | bytes 262160
  214.6 77.7 %reduce-scatter.6.cloned.1.call-done = bf16[256,2048]{1,0:T(8,128)(2,1)} async-done(((bf16[256,8192]{1,0:T(8,128)(2,1)}), bf16[256,2048]{1,0:T(8,128)(2,1)}) %reduce-scatter.6.cloned.1.call-update) | async-done | bytes 1048592 | tf_op jit(solution)/shard_map/reduce_scatter | solution.py:88
  (114 shorter events, 62.5 us)
Async XLA Ops:
  7.2 29.5 %all-gather.3.cloned.1.call-start = ((), (), s32[]{:S(2)}) async-start(), calls=%async_computation.2 | async-start | bytes 1179648 | tf_op jit(solution)/shard_map/all_gather | solution.py:65
  8.8 53.9 %all-gather.5.cloned.1.call-start = ((), (), s32[]{:S(2)}) async-start(), calls=%async_computation.3 | async-start | bytes 1179648 | tf_op jit(solution)/shard_map/all_gather | solution.py:66
  10.5 202.3 %reduce-scatter.8.cloned.1.call-start = ((), (), s32[]{:S(2)}) async-start(), calls=%async_computation.5 | async-start | bytes 2359296
  28.8 3.7 %copy-start.6 = (s32[2048]{0:T(1024)S(1)}, s32[2048]{0:T(1024)}, u32[]{:S(2)}) copy-start(s32[2048]{0:T(1024)} %param.13) | copy-start | bytes 24580
  30.3 1.0 copy-start
  65.3 1.8 copy-start.2
  71.2 1.3 copy-start.3
  75.1 1.8 copy-start.2
  81.0 1.3 copy-start.3
  84.9 1.8 copy-start.2
  90.8 1.3 copy-start.3
  94.7 1.8 copy-start.2
  100.6 1.3 copy-start.3
  101.9 2.8 copy-start.1
  108.0 2.3 copy-start.5
  121.8 2.3 copy-start.5
  135.7 2.3 copy-start.5
  149.6 2.3 copy-start.5
  167.1 4.3 %copy-start.4 = (bf16[2,8,256,128]{3,2,1,0:T(8,128)(2,1)S(1)}, bf16[2,8,256,128]{3,2,1,0:T(8,128)(2,1)}, u32[]{:S(2)}) copy-start(bf16[2,8,256,128]{3,2,1,0:T(8,128)(2,1)} %get-tuple-element.366) | copy-start | bytes 3145732
  171.4 121.0 %reduce-scatter.6.cloned.1.call-start = ((), (), s32[]{:S(2)}) async-start(), calls=%async_computation.4 | async-start | bytes 5242880 | tf_op jit(solution)/shard_map/reduce_scatter | solution.py:88
Sparse Core Ops, SparseCore 0:
  10.5 26.1 all-gather.2
  39.2 23.4 all-gather.4
  171.5 41.1 reduce-scatter.7
  215.6 76.7 reduce-scatter.5
where the time goes:
time: 300 us; the launch traced here: 299 us
  waiting for transfers between devices  130 us (43%)
  matrix products  106 us (35%)
  local copies, waits for them, and re-layouts  29.7 us (10%)
  other arithmetic  16.1 us (5%)
  between operations  13.9 us (5%)
  loops' own time  3.36 us (1%)
    reduce_scatter x1, waiting for transfers between devices, local(): lax.psum_scatter(partial_out, 'tp', scatter_dimension=1, tiled=True)  77.7 us
    all_gather x1, waiting for transfers between devices, local(): lax.all_gather(values, 'ctx', axis=0, tiled=True)  26 us
    unnamed x5, waiting for transfers between devices  21.8 us
    dot_general x8, matrix products, masked_scores(): jnp.einsum('rngd,knd->ngrk', qgroups, key_block, preferred_element_type=j...  18.5 us
    dot_general x1, matrix products, local(): jnp.einsum('ngrd,ngde->re', attended, weight_grid, preferred_element_type...  17.5 us
    dot_general x1, matrix products, local(): lax.dot_general(grad_out, out_weight, (((1,), (1,)), ((), ())), preferred...  16.7 us
    dot_general x4, matrix products, online_step(): jnp.einsum('ngrk,knd->ngrd', weights.astype(jnp.bfloat16), value_block, p...  16.5 us
    dot_general x4, matrix products, block_grads(): jnp.einsum('rngd,knd->ngrk', grad_groups, value_block, preferred_element_...  15.2 us
  transfers between devices with their start and end apart: 4, of which 4 were waited for; matrix products, arithmetic and copies ran while one was open for 15% of the time, Pallas kernels for 0%

commit v1 on v0

v1 whole, which is shorter than its diff:
```python
import functools
import math

import jax
import jax.numpy as jnp
from jax import lax
from jax.experimental import pallas as pl
from jax.experimental.pallas import tpu as pltpu
from jax.sharding import PartitionSpec as P

NEG_FILL = -1e30
LOG2E = 1.4426950408889634
PAIR = 256
COLS = 256
F32 = jnp.float32
BF16 = jnp.bfloat16
VMEM_LIMIT = 50 * 1024 * 1024


def dot(a, b):
    return jnp.dot(a, b, preferred_element_type=F32)


def scores_t(k_tile, qt_part, scale):
    return dot(k_tile, qt_part) * scale


def mask_t(scores, key_start, query_start, span):
    key_pos = key_start + lax.broadcasted_iota(jnp.int32, scores.shape, 0)
    query_pos = query_start + lax.broadcasted_iota(jnp.int32, scores.shape, 1) % span
    return jnp.where(key_pos <= query_pos, scores, NEG_FILL)


def load_sorted(info_ref, src_ref, blocks, span):
    for j in range(blocks):
        stored = info_ref[j]
        yield j, src_ref[stored // 2, 0, stored % 2]


def forward_kernel(blocks, span, scale, info_ref, q_ref, k_ref, v_ref, att_ref, att_t_ref, lse_ref,
                   k_sorted, v_t, q_t, out_t, top, total):
    half = pl.program_id(1)
    heads = q_ref.shape[1] // span
    query_block = info_ref[blocks + half]

    @pl.when(half == 0)
    def _():
        for j, block in load_sorted(info_ref, k_ref, blocks, span):
            k_sorted[j * span:(j + 1) * span, :] = block
        for j, block in load_sorted(info_ref, v_ref, blocks, span):
            v_t[:, j * span:(j + 1) * span] = block.T

    for h in range(heads):
        q_t[:, h * span:(h + 1) * span] = q_ref[:, h * span:(h + 1) * span].T
    out_t[...] = jnp.zeros_like(out_t)
    top[...] = jnp.full_like(top, NEG_FILL)
    total[...] = jnp.zeros_like(total)

    def step(j, masked):
        start = pl.multiple_of(j * PAIR, PAIR)
        k_tile = k_sorted[pl.ds(start, PAIR), :]
        v_tile = v_t[:, pl.ds(start, PAIR)]
        for c in range(0, q_t.shape[1], COLS):
            cols = slice(c, c + COLS)
            scores = scores_t(k_tile, q_t[:, cols], scale)
            if masked:
                scores = mask_t(scores, start, query_block * span, span)
            old_top = top[:, cols]
            new_top = jnp.maximum(old_top, jnp.max(scores, axis=0, keepdims=True))
            weights = jnp.exp2(scores - new_top)
            factor = jnp.exp2(old_top - new_top)
            top[:, cols] = new_top
            total[:, cols] = total[:, cols] * factor + jnp.sum(weights, axis=0, keepdims=True)
            out_t[:, cols] = out_t[:, cols] * factor + dot(v_tile, weights.astype(BF16))

    last = query_block // 2
    pl.loop(0, last)(lambda j: step(j, False))
    step(last, True)

    lse_ref[0, 0] = top[...] + jnp.log2(total[...])
    inverse = 1.0 / total[...]
    for h in range(heads):
        cols = slice(h * span, (h + 1) * span)
        part = out_t[:, cols] * inverse[:, cols]
        att_t_ref[0, 0, :, cols] = part.astype(BF16)
        att_ref[:, cols] = part.T.astype(BF16)


def backward_kernel(blocks, span, scale, out_scale, info_ref, q_ref, go_ref, k_ref, v_ref, att_t_ref,
                    lse_ref, gq_ref, gkv_ref, k_sorted, v_sorted, k_t, q_s, q_t, go_s, go_t, gq_t,
                    delta, gk, gv):
    half = pl.program_id(0)
    heads = q_ref.shape[1] // span
    query_block = info_ref[blocks + half]

    @pl.when(half == 0)
    def _():
        for j, block in load_sorted(info_ref, k_ref, blocks, span):
            k_sorted[j * span:(j + 1) * span, :] = block
            k_t[:, j * span:(j + 1) * span] = block.T
        for j, block in load_sorted(info_ref, v_ref, blocks, span):
            v_sorted[j * span:(j + 1) * span, :] = block
        gk[...] = jnp.zeros_like(gk)
        gv[...] = jnp.zeros_like(gv)

    for h in range(heads):
        part = slice(h * span, (h + 1) * span)
        q_s[part, :] = q_ref[:, part]
        q_t[:, part] = q_ref[:, part].T
        go_s[part, :] = go_ref[:, part]
        turned = go_ref[:, part].T
        go_t[:, part] = turned
        delta[:, part] = jnp.sum(
            att_t_ref[0, 0, :, part].astype(F32) * turned.astype(F32), axis=0, keepdims=True
        )
    gq_t[...] = jnp.zeros_like(gq_t)

    def step(j, masked):
        start = pl.multiple_of(j * PAIR, PAIR)
        rows = pl.ds(start, PAIR)
        k_tile = k_sorted[rows, :]
        v_tile = v_sorted[rows, :]
        kt_tile = k_t[:, rows]
        all_w, all_d = [], []
        for c in range(0, q_t.shape[1], COLS):
            cols = slice(c, c + COLS)
            scores = scores_t(k_tile, q_t[:, cols], scale)
            if masked:
                scores = mask_t(scores, start, query_block * span, span)
            weights = jnp.exp2(scores - lse_ref[0, 0, :, cols])
            dweights = dot(v_tile, go_t[:, cols])
            dscores = (weights * (dweights - delta[:, cols])).astype(BF16)
            gq_t[:, cols] += dot(kt_tile, dscores)
            all_w.append(weights.astype(BF16))
            all_d.append(dscores)
        gv[rows, :] += dot(jnp.concatenate(all_w, axis=1), go_s[...])
        gk[rows, :] += dot(jnp.concatenate(all_d, axis=1), q_s[...])

    last = query_block // 2
    pl.loop(0, last)(lambda j: step(j, False))
    step(last, True)

    for h in range(heads):
        part = slice(h * span, (h + 1) * span)
        gq_ref[:, part] = (gq_t[:, part] * out_scale).T.astype(BF16)

    @pl.when(half == 1)
    def _():
        for j in range(blocks):
            stored = info_ref[j]
            part = slice(j * span, (j + 1) * span)
            gkv_ref[stored // 2, 0, stored % 2] = (gk[part, :] * out_scale).astype(BF16)
            gkv_ref[stored // 2, 1, stored % 2] = gv[part, :].astype(BF16)


def project_kernel(info_ref, a_ref, w_ref, o_ref):
    o_ref[...] = dot(a_ref[...], w_ref[...]).astype(BF16)


def project(first, attended, weight, width):
    rows, depth = attended.shape
    tile = 512
    return pl.pallas_call(
        project_kernel,
        out_shape=jax.ShapeDtypeStruct((rows, width), BF16),
        grid_spec=pltpu.PrefetchScalarGridSpec(
            num_scalar_prefetch=1,
            grid=(width // tile,),
            in_specs=[
                pl.BlockSpec((rows, depth), lambda i, info: (0, 0)),
                pl.BlockSpec((depth, tile), lambda i, info: (0, info[0] * (width // tile) + i)),
            ],
            out_specs=pl.BlockSpec((rows, tile), lambda i, info: (0, i)),
        ),
        compiler_params=pltpu.CompilerParams(vmem_limit_bytes=VMEM_LIMIT),
        cost_estimate=pl.CostEstimate(
            flops=2 * rows * depth * width, bytes_accessed=2 * depth * width, transcendentals=0
        ),
    )(first, attended, weight)


def forward(info, q2, kv_all, span):
    rows, flat = q2.shape
    ctx, kv2, _, _, hd = kv_all.shape
    kvl = kv2 // 2
    blocks = ctx * 2
    seq = blocks * span
    width = flat // kvl
    kernel = functools.partial(forward_kernel, blocks, span, LOG2E / math.sqrt(hd))
    work = rows * seq * flat // 2
    return pl.pallas_call(
        kernel,
        out_shape=(
            jax.ShapeDtypeStruct((rows, flat), BF16),
            jax.ShapeDtypeStruct((kvl, 2, hd, width), BF16),
            jax.ShapeDtypeStruct((kvl, 2, 1, width), F32),
        ),
        grid_spec=pltpu.PrefetchScalarGridSpec(
            num_scalar_prefetch=1,
            grid=(kvl, 2),
            in_specs=[
                pl.BlockSpec((span, width), lambda g, i, info: (i, g)),
                pl.BlockSpec((ctx, 1, 2, span, hd), lambda g, i, info: (0, g, 0, 0, 0)),
                pl.BlockSpec((ctx, 1, 2, span, hd), lambda g, i, info: (0, kvl + g, 0, 0, 0)),
            ],
            out_specs=(
                pl.BlockSpec((span, width), lambda g, i, info: (i, g)),
                pl.BlockSpec((1, 1, hd, width), lambda g, i, info: (g, i, 0, 0)),
                pl.BlockSpec((1, 1, 1, width), lambda g, i, info: (g, i, 0, 0)),
            ),
            scratch_shapes=[
                pltpu.VMEM((seq, hd), BF16),
                pltpu.VMEM((hd, seq), BF16),
                pltpu.VMEM((hd, width), BF16),
                pltpu.VMEM((hd, width), F32),
                pltpu.VMEM((1, width), F32),
                pltpu.VMEM((1, width), F32),
            ],
        ),
        compiler_params=pltpu.CompilerParams(vmem_limit_bytes=VMEM_LIMIT),
        cost_estimate=pl.CostEstimate(
            flops=8 * work, bytes_accessed=4 * rows * flat, transcendentals=work // hd
        ),
    )(info, q2, kv_all, kv_all)


def backward(info, q2, go2, kv_all, att_t, lse, span, g):
    rows, flat = q2.shape
    ctx, kv2, _, _, hd = kv_all.shape
    kvl = kv2 // 2
    blocks = ctx * 2
    seq = blocks * span
    width = flat // kvl
    kernel = functools.partial(
        backward_kernel, blocks, span, LOG2E / math.sqrt(hd), 1.0 / math.sqrt(hd)
    )
    work = rows * seq * width // 2
    return pl.pallas_call(
        kernel,
        out_shape=(
            jax.ShapeDtypeStruct((rows, width), BF16),
            jax.ShapeDtypeStruct((ctx, 2, 2, span, hd), BF16),
        ),
        grid_spec=pltpu.PrefetchScalarGridSpec(
            num_scalar_prefetch=1,
            grid=(2,),
            in_specs=[
                pl.BlockSpec((span, width), lambda i, info: (i, g)),
                pl.BlockSpec((span, width), lambda i, info: (i, g)),
                pl.BlockSpec((ctx, 1, 2, span, hd), lambda i, info: (0, g, 0, 0, 0)),
                pl.BlockSpec((ctx, 1, 2, span, hd), lambda i, info: (0, kvl + g, 0, 0, 0)),
                pl.BlockSpec((1, 1, hd, width), lambda i, info: (g, i, 0, 0)),
                pl.BlockSpec((1, 1, 1, width), lambda i, info: (g, i, 0, 0)),
            ],
            out_specs=(
                pl.BlockSpec((span, width), lambda i, info: (i, 0)),
                pl.BlockSpec((ctx, 2, 2, span, hd), lambda i, info: (0, 0, 0, 0, 0)),
            ),
            scratch_shapes=[
                pltpu.VMEM((seq, hd), BF16),
                pltpu.VMEM((seq, hd), BF16),
                pltpu.VMEM((hd, seq), BF16),
                pltpu.VMEM((width, hd), BF16),
                pltpu.VMEM((hd, width), BF16),
                pltpu.VMEM((width, hd), BF16),
                pltpu.VMEM((hd, width), BF16),
                pltpu.VMEM((hd, width), F32),
                pltpu.VMEM((1, width), F32),
                pltpu.VMEM((seq, hd), F32),
                pltpu.VMEM((seq, hd), F32),
            ],
        ),
        compiler_params=pltpu.CompilerParams(vmem_limit_bytes=VMEM_LIMIT),
        cost_estimate=pl.CostEstimate(
            flops=20 * work, bytes_accessed=4 * rows * flat, transcendentals=work // hd
        ),
    )(info, q2, go2, kv_all, kv_all, att_t, lse)


def local(queries, keys, values, positions, out_weight, grad_out):
    rows, heads, hd = queries.shape
    kvl = keys.shape[1]
    span = rows // 2
    ctx = lax.axis_size("ctx")
    tp = lax.axis_size("tp")
    me = lax.axis_index("tp")
    seq = rows * ctx
    blocks = 2 * ctx
    model = out_weight.shape[1]
    chunk = model // tp

    kv = jnp.stack([keys, values]).transpose(0, 2, 1, 3).reshape(2 * kvl, 2, span, hd)
    kv_all = lax.all_gather(kv, "ctx", axis=0, tiled=False)

    block_of = positions.reshape(blocks, span)[:, 0] // span
    order = jnp.arange(blocks, dtype=jnp.int32)
    place = jnp.sum(jnp.where(block_of[None, :] == order[:, None], order[None, :], 0), axis=1)
    mine = lax.dynamic_slice_in_dim(block_of, 2 * lax.axis_index("ctx"), 2)
    info = jnp.concatenate([place, mine]).astype(jnp.int32)

    q2 = queries.reshape(rows, heads * hd)
    grad_heads = lax.dot_general(
        grad_out, out_weight, (((1,), (1,)), ((), ())), preferred_element_type=F32
    ).astype(BF16)

    attended, att_t, lse = forward(info, q2, kv_all, span)

    early = jnp.where(me < (tp + 1) // 2, tp - 1, 0).astype(jnp.int32).reshape(1)
    first = project(early, attended, out_weight, chunk)
    partial_out = project(jnp.zeros((1,), jnp.int32), attended, out_weight, model)

    def own_part(index):
        index = jnp.clip(index, 0, tp - 1)
        return lax.dynamic_slice_in_dim(partial_out, index * chunk, chunk, axis=1)

    right = left = first
    for k in range(tp - 1):
        to_right = [(z, z + 1) for z in range(tp - 1) if z <= k]
        to_left = [(tp - 1 - a, tp - 1 - b) for a, b in to_right]
        from_left = lax.ppermute(right, "tp", to_right).astype(F32)
        from_right = lax.ppermute(left, "tp", to_left).astype(F32)
        if k < tp - 2:
            right = (own_part(tp - 2 - k + me).astype(F32) + from_left).astype(BF16)
            left = (own_part(k + 2 - tp + me).astype(F32) + from_right).astype(BF16)
    layer_out = (own_part(me).astype(F32) + from_left + from_right).astype(BF16)

    query_parts, kv_parts = [], []
    for g in range(kvl):
        gq, gkv = backward(info, q2, grad_heads, kv_all, att_t, lse, span, g)
        query_parts.append(gq)
        kv_parts.append(gkv)
    grad_queries = jnp.concatenate(query_parts, axis=1).reshape(rows, heads, hd)
    terms = jnp.stack(kv_parts, axis=1).reshape(ctx, kvl, 2, rows, hd)
    owned = lax.psum_scatter(terms, "ctx", scatter_dimension=0, tiled=False)
    return (
        layer_out,
        grad_queries,
        owned[:, 0].transpose(1, 0, 2),
        owned[:, 1].transpose(1, 0, 2),
    )


def solution(mesh):
    placed = (
        P("ctx", "tp", None),
        P("ctx", "tp", None),
        P("ctx", "tp", None),
        P(),
        P("tp", None),
        P("ctx", None),
    )
    return jax.shard_map(
        local,
        mesh=mesh,
        in_specs=placed,
        out_specs=(
            P("ctx", "tp"),
            P("ctx", "tp", None),
            P("ctx", "tp", None),
            P("ctx", "tp", None),
        ),
        check_vma=False,
    )
```

time: 300 us -> 223 us (0.74)
  matrix products: 106 us -> 16.6 us
  Pallas kernels: 0 us -> 82.5 us
  waiting for transfers between devices: 130 us -> 73 us
  local copies, waits for them, and re-layouts: 29.7 us -> 7.22 us
  starting transfers between devices: 0.16 us -> 12.7 us
  loops' own time: 3.36 us -> 0 us
    dot_general x29 -> x0, matrix products: 89.4 us -> none  [the longest x8 18.5 us: masked_scores(): jnp.einsum('rngd,knd->ngrk', qgroups, key_block, preferred_element_type=j...]
    pallas_call x0 -> x5, Pallas kernels: none -> 82.5 us  [the longest x2 29.8 us: backward(): pl.pallas_call(kernel, out_shape=(jax.ShapeDtypeStruct((rows, width), BF1...]
    reduce_scatter x1, waiting for transfers between devices: 77.7 us -> 27.2 us  [local(): owned = lax.psum_scatter(terms, 'ctx', scatter_dimension=0, tiled=False)]
    unnamed x5 -> x2, waiting for transfers between devices: 21.8 us -> 0.03 us
    ppermute x0 -> x6, waiting for transfers between devices: none -> 16 us  [the longest x3 16 us: local(): from_right = lax.ppermute(left, 'tp', to_left).astype(F32)]
    ppermute x0 -> x6, starting transfers between devices: none -> 12.6 us  [the longest x3 8.98 us: local(): from_left = lax.ppermute(right, 'tp', to_right).astype(F32)]
    convert_element_type x1 -> x4, other arithmetic: 0.24 us -> 12.8 us  [the longest x2 7.4 us: local(): right = (own_part(tp - 2 - k + me).astype(F32) + from_left).astype(BF16)]
    unnamed x15 -> x10, local copies, waits for them, and re-layouts: 13.6 us -> 5.3 us
  transfers between devices with their start and end apart: 4 -> 8, of which waited for: 4 -> 3; matrix products, arithmetic and copies ran while one was open for 15% -> 15% of each run, Pallas kernels for 0% -> 23%
where the time goes in v1:
time: 223 us; the launch traced here: 222 us
  Pallas kernels  82.5 us (37%)
  waiting for transfers between devices  73 us (33%)
  matrix products  16.6 us (7%)
  other arithmetic  15.9 us (7%)
  between operations  14.2 us (6%)
  starting transfers between devices  12.7 us (6%)
  local copies, waits for them, and re-layouts  7.22 us (3%)
    pallas_call x2, Pallas kernels, backward(): pl.pallas_call(kernel, out_shape=(jax.ShapeDtypeStruct((rows, width), BF1...  29.8 us
    all_gather x1, waiting for transfers between devices, local(): kv_all = lax.all_gather(kv, 'ctx', axis=0, tiled=False)  29.8 us
    reduce_scatter x1, waiting for transfers between devices, local(): owned = lax.psum_scatter(terms, 'ctx', scatter_dimension=0, tiled=False)  27.2 us
    pallas_call x2, Pallas kernels, project(): pl.pallas_call(project_kernel, out_shape=jax.ShapeDtypeStruct((rows, widt...  27.2 us
    pallas_call x1, Pallas kernels, forward(): pl.pallas_call(kernel, out_shape=(jax.ShapeDtypeStruct((rows, flat), BF16...  25.5 us
    dot_general x1, matrix products, local(): lax.dot_general(grad_out, out_weight, (((1,), (1,)), ((), ())), preferred...  16.6 us
    ppermute x3, waiting for transfers between devices, local(): from_right = lax.ppermute(left, 'tp', to_left).astype(F32)  16 us
    ppermute x3, starting transfers between devices, local(): from_left = lax.ppermute(right, 'tp', to_right).astype(F32)  8.98 us
  transfers between devices with their start and end apart: 8, of which 3 were waited for; matrix products, arithmetic and copies ran while one was open for 15% of the time, Pallas kernels for 23%

profile of v1, /device:TPU:0, one launch (start us, length us, event | category | flops | bytes accessed | tf_op | source)
XLA Modules:
  0.0 222.3 jit_solution(2022087320861721656)
XLA Ops:
  7.2 1.4 maximum_bitcast_fusion.1
  9.4 1.5 copy.32
  11.3 29.8 %all-gather.2.cloned.1.call-done.k_ref.v_ref = bf16[8,4,2,128,128]{4,3,2,1,0:T(8,128)(2,1)} async-done(((bf16[1,4,2,128,128]{4,3,2,1,0:T(8,128)(2,1)}), bf16[8,4,2,128,128]{4,3,2,1,0:T(8,128)(2,1)}) %all-gather.2.cloned.1.call-update) | async-done | bytes 2097168 | tf_op jit(solution)/shard_map/all_gather | solution.py:293
  41.1 25.5 %shard_map.93 = (bf16[256,2048]{1,0:T(8,128)(2,1)S(1)}, bf16[2,2,128,1024]{3,2,1,0:T(8,128)(2,1)S(1)}, f32[2,2,1,1024]{3,2,1,0:T(1,128)S(1)}) custom-call(s32[18]{0:T(128)S(1)} %pad_add_fusion.info_ref, bf16[256,2048]{1,0:T(8,128)(2,1)S(1)} %bitcast.31, bf16[8,4,2,128,128]{4,3,2,1,0:T(8,128)(2,1)} %all-gather.2.cloned.1.call-done.k_ref.v_ref, ...), custom_call_target="tpu_custom_call" | custom-call | flops 4294967296 | bytes 2097152 | tf_op jit(solution)/shard_map/pallas_call | solution.py:191
  66.6 1.0 copy-done
  67.6 5.5 %shard_map.95 = bf16[256,2048]{1,0:T(8,128)(2,1)S(1)} custom-call(s32[1]{0:T(128)} %bitcast.5.info_ref, bf16[256,2048]{1,0:T(8,128)(2,1)S(1)} %get-tuple-element.11.a_ref, bf16[2048,8192]{1,0:T(8,128)(2,1)} %w_ref.3), custom_call_target="tpu_custom_call" | custom-call | flops 2147483648 | bytes 8388608 | tf_op jit(solution)/shard_map/pallas_call | solution.py:163
  73.2 4.5 %collective-permute-start = (bf16[256,2048]{1,0:T(8,128)(2,1)S(1)}, bf16[256,2048]{1,0:T(8,128)(2,1)}, u32[]{:S(2)}, u32[]{:S(2)}) collective-permute-start(bf16[256,2048]{1,0:T(8,128)(2,1)S(1)} %shard_map.95), channel_id=1, source_target_pairs={{0,1},{4,5},{8,9},{12,13},{16,17},{20,21},{24,25},{28,29}} | collective-permute-start | bytes 3145736 | tf_op jit(solution)/shard_map/ppermute | solution.py:320
  77.6 16.6 %convolution_convert_fusion.go_ref = bf16[256,2048]{1,0:T(8,128)(2,1)} fusion(bf16[256,8192]{1,0:T(8,128)(2,1)} %param.11, bf16[2048,8192]{1,0:T(8,128)(2,1)} %w_ref.3), kind=kOutput, calls=%fused_computation | convolution fusion | flops 8590458880 | bytes 38797312 | tf_op jit(solution)/shard_map/dot_general | solution.py:302
  94.3 1.7 collective-permute-start.3
  95.9 21.7 %shard_map.94 = bf16[256,8192]{1,0:T(8,128)(2,1)} custom-call(s32[1]{0:T(128)} %constant.15.clone.1.info_ref, bf16[256,2048]{1,0:T(8,128)(2,1)S(1)} %get-tuple-element.11.a_ref, bf16[2048,8192]{1,0:T(8,128)(2,1)} %w_ref.3), custom_call_target="tpu_custom_call" | custom-call | flops 8589934592 | bytes 33554432 | tf_op jit(solution)/shard_map/pallas_call | solution.py:163
  117.6 3.0 %add_convert_fusion.4 = bf16[256,2048]{1,0:T(8,128)(2,1)} fusion(bf16[256,2048]{1,0:T(8,128)(2,1)} %collective-permute-done, bf16[256,8192]{1,0:T(8,128)(2,1)} %shard_map.94, s32[]{:T(128)S(6)} %select_n.40), kind=kLoop, calls=%fused_computation.6 | loop fusion | flops 2097152 | bytes 3145732 | tf_op jit(solution)/shard_map/convert_element_type | solution.py:323
  120.6 2.4 %collective-permute-start.1 = (bf16[256,2048]{1,0:T(8,128)(2,1)}, bf16[256,2048]{1,0:T(8,128)(2,1)}, u32[]{:S(2)}, u32[]{:S(2)}) collective-permute-start(bf16[256,2048]{1,0:T(8,128)(2,1)} %add_convert_fusion.4), channel_id=1, source_target_pairs={{0,1},{1,2},{4,5},{5,6},{8,9},{9,10},{12,13},{13,14},{16,17},{17,1... | collective-permute-start | bytes 3145736 | tf_op jit(solution)/shard_map/ppermute | solution.py:320
  123.0 14.9 %shard_map.97 = (bf16[256,1024]{1,0:T(8,128)(2,1)S(1)}, bf16[8,2,2,128,128]{4,3,2,1,0:T(8,128)(2,1)S(1)}) custom-call(s32[18]{0:T(128)S(1)} %pad_add_fusion.info_ref, bf16[256,2048]{1,0:T(8,128)(2,1)S(1)} %bitcast.32, bf16[256,2048]{1,0:T(8,128)(2,1)S(1)} %copy-done.1, bf16[8,4,2,128,128]{4,3,2,1,0:T(8,128)(2,1)} %all-gather.2.cloned.1.call-done.k_ref.v_ref, ...), custom_call_target="tpu_custom_call" | custom-call | flops 5368709120 | bytes 2097152 | tf_op jit(solution)/shard_map/pallas_call | solution.py:238
  137.9 14.9 %shard_map.96 = (bf16[256,1024]{1,0:T(8,128)(2,1)S(1)}, bf16[8,2,2,128,128]{4,3,2,1,0:T(8,128)(2,1)S(1)}) custom-call(s32[18]{0:T(128)S(1)} %pad_add_fusion.info_ref, bf16[256,2048]{1,0:T(8,128)(2,1)S(1)} %bitcast.33, bf16[256,2048]{1,0:T(8,128)(2,1)S(1)} %copy-done.1, bf16[8,4,2,128,128]{4,3,2,1,0:T(8,128)(2,1)} %all-gather.2.cloned.1.call-done.k_ref.v_ref, ...), custom_call_target="tpu_custom_call" | custom-call | flops 5368709120 | bytes 2097152 | tf_op jit(solution)/shard_map/pallas_call | solution.py:238
  152.8 1.5 pad_maximum_fusion
  154.3 4.4 %add_convert_fusion.3 = (bf16[256,2048]{1,0:T(8,128)(2,1)}, bf16[256,2048]{1,0:T(8,128)(2,1)}) fusion(bf16[256,2048]{1,0:T(8,128)(2,1)} %collective-permute-done.1, bf16[256,8192]{1,0:T(8,128)(2,1)} %shard_map.94, s32[]{:T(128)S(6)} %select_n.39, bf16[256,2048]{1,0:T(8,128)(2,1)} %collective-permute-done.3, s32[]{:T(128)S(6)} %select_n.43), kind=kLoop, calls=%fused_computation.5 | loop fusion | flops 4194304 | bytes 6291464 | tf_op jit(solution)/shard_map/convert_element_type | solution.py:323
  159.5 2.2 collective-permute-start.2
  161.7 2.7 %add_convert_fusion.1 = bf16[256,2048]{1,0:T(8,128)(2,1)} fusion(bf16[256,2048]{1,0:T(8,128)(2,1)S(1)} %collective-permute-done.4, bf16[256,8192]{1,0:T(8,128)(2,1)} %shard_map.94, s32[]{:T(128)S(6)} %select_n.42), kind=kLoop, calls=%fused_computation.3 | loop fusion | flops 2097152 | bytes 3145732 | tf_op jit(solution)/shard_map/convert_element_type | solution.py:324
  164.3 1.3 collective-permute-start.5
  165.7 1.2 copy.30
  166.9 27.2 %reduce-scatter.2.cloned.1.call-done = bf16[1,2,2,256,128]{4,3,2,1,0:T(8,128)(2,1)} async-done(((bf16[8,2,2,256,128]{4,3,2,1,0:T(8,128)(2,1)}), bf16[1,2,2,256,128]{4,3,2,1,0:T(8,128)(2,1)}) %reduce-scatter.2.cloned.1.call-update) | async-done | bytes 262160 | tf_op jit(solution)/shard_map/reduce_scatter | solution.py:334
  194.1 1.0 slice_bitcast_fusion
  196.7 16.0 %collective-permute-done.5 = bf16[256,2048]{1,0:T(8,128)(2,1)S(1)} collective-permute-done((bf16[256,2048]{1,0:T(8,128)(2,1)}, bf16[256,2048]{1,0:T(8,128)(2,1)S(1)}, u32[]{:S(2)}, u32[]{:S(2)}) %collective-permute-start.5) | collective-permute-done | bytes 1048608 | tf_op jit(solution)/shard_map/ppermute | solution.py:321
  212.7 2.7 %add_convert_fusion = bf16[256,2048]{1,0:T(8,128)(2,1)} fusion(bf16[256,2048]{1,0:T(8,128)(2,1)S(1)} %collective-permute-done.5, bf16[256,2048]{1,0:T(8,128)(2,1)S(1)} %collective-permute-done.2, bf16[256,8192]{1,0:T(8,128)(2,1)} %shard_map.94, s32[]{:T(128)S(6)} %select_n.38), kind=kLoop, calls=%fused_computation.2 | loop fusion | flops 3145728 | bytes 4194308 | tf_op jit(solution)/shard_map/convert_element_type | solution.py:325
  (24 shorter events, 3.6 us)
Async XLA Ops:
  7.2 3.8 %copy-start.2 = (s32[2048]{0:T(1024)S(1)}, s32[2048]{0:T(1024)}, u32[]{:S(2)}) copy-start(s32[2048]{0:T(1024)} %param.9) | copy-start | bytes 24580
  7.2 33.9 %all-gather.2.cloned.1.call-start = ((), (), s32[]{:S(2)}) async-start(), calls=%async_computation.1 | async-start | bytes 2359296 | tf_op jit(solution)/shard_map/all_gather | solution.py:293
  9.3 184.8 %reduce-scatter.2.cloned.1.call-start = ((), (), s32[]{:S(2)}) async-start(), calls=%async_computation.2 | async-start | bytes 2359296 | tf_op jit(solution)/shard_map/reduce_scatter | solution.py:334
  66.6 1.0 copy-start
  73.2 44.5 %collective-permute-start = (bf16[256,2048]{1,0:T(8,128)(2,1)S(1)}, bf16[256,2048]{1,0:T(8,128)(2,1)}, u32[]{:S(2)}, u32[]{:S(2)}) collective-permute-start(bf16[256,2048]{1,0:T(8,128)(2,1)S(1)} %shard_map.95), channel_id=1, source_target_pairs={{0,1},{4,5},{8,9},{12,13},{16,17},{20,21},{24,25},{28,29}} | collective-permute-start | bytes 3145736 | tf_op jit(solution)/shard_map/ppermute | solution.py:320
  94.3 60.0 %collective-permute-start.3 = (bf16[256,2048]{1,0:T(8,128)(2,1)S(1)}, bf16[256,2048]{1,0:T(8,128)(2,1)}, u32[]{:S(2)}, u32[]{:S(2)}) collective-permute-start(bf16[256,2048]{1,0:T(8,128)(2,1)S(1)} %shard_map.95), channel_id=1, source_target_pairs={{3,2},{7,6},{11,10},{15,14},{19,18},{23,22},{27,26},{31,30}} | collective-permute-start | bytes 3145736 | tf_op jit(solution)/shard_map/ppermute | solution.py:321
  117.6 5.4 %copy-start.1 = (bf16[256,2048]{1,0:T(8,128)(2,1)S(1)}, bf16[256,2048]{1,0:T(8,128)(2,1)}, u32[]{:S(2)}) copy-start(bf16[256,2048]{1,0:T(8,128)(2,1)} %convolution_convert_fusion.go_ref) | copy-start | bytes 3145732
  120.6 33.7 %collective-permute-start.1 = (bf16[256,2048]{1,0:T(8,128)(2,1)}, bf16[256,2048]{1,0:T(8,128)(2,1)}, u32[]{:S(2)}, u32[]{:S(2)}) collective-permute-start(bf16[256,2048]{1,0:T(8,128)(2,1)} %add_convert_fusion.4), channel_id=1, source_target_pairs={{0,1},{1,2},{4,5},{5,6},{8,9},{9,10},{12,13},{13,14},{16,17},{17,1... | collective-permute-start | bytes 3145736 | tf_op jit(solution)/shard_map/ppermute | solution.py:320
  158.7 2.9 %collective-permute-start.4 = (bf16[256,2048]{1,0:T(8,128)(2,1)}, bf16[256,2048]{1,0:T(8,128)(2,1)S(1)}, u32[]{:S(2)}, u32[]{:S(2)}) collective-permute-start(bf16[256,2048]{1,0:T(8,128)(2,1)} %get-tuple-element.27), channel_id=1, source_target_pairs={{3,2},{2,1},{7,6},{6,5},{11,10},{10,9},{15,14},{14,13},{19,18},{18... | collective-permute-start | bytes 3145736 | tf_op jit(solution)/shard_map/ppermute | solution.py:321
  159.5 37.2 %collective-permute-start.2 = (bf16[256,2048]{1,0:T(8,128)(2,1)}, bf16[256,2048]{1,0:T(8,128)(2,1)S(1)}, u32[]{:S(2)}, u32[]{:S(2)}) collective-permute-start(bf16[256,2048]{1,0:T(8,128)(2,1)} %get-tuple-element.26), channel_id=1, source_target_pairs={{0,1},{1,2},{2,3},{4,5},{5,6},{6,7},{8,9},{9,10},{10,11},{12,13},{... | collective-permute-start | bytes 3145736 | tf_op jit(solution)/shard_map/ppermute | solution.py:320
  164.3 48.4 %collective-permute-start.5 = (bf16[256,2048]{1,0:T(8,128)(2,1)}, bf16[256,2048]{1,0:T(8,128)(2,1)S(1)}, u32[]{:S(2)}, u32[]{:S(2)}) collective-permute-start(bf16[256,2048]{1,0:T(8,128)(2,1)} %add_convert_fusion.1), channel_id=1, source_target_pairs={{3,2},{2,1},{1,0},{7,6},{6,5},{5,4},{11,10},{10,9},{9,8},{15,14},{... | collective-permute-start | bytes 3145736 | tf_op jit(solution)/shard_map/ppermute | solution.py:321
Sparse Core Ops, SparseCore 0:
  10.5 30.5 all-gather.1
  154.4 39.6 reduce-scatter.1

commit v2 on v1

--- a/solution.py
+++ b/solution.py
@@ -11,7 +11,8 @@
 NEG_FILL = -1e30
 LOG2E = 1.4426950408889634
 PAIR = 256
-COLS = 256
+FORWARD_COLS = 512
+BACKWARD_COLS = 256
 F32 = jnp.float32
 BF16 = jnp.bfloat16
 VMEM_LIMIT = 50 * 1024 * 1024
@@ -19,16 +20,22 @@
 
 def dot(a, b):
     return jnp.dot(a, b, preferred_element_type=F32)
-
-
-def scores_t(k_tile, qt_part, scale):
-    return dot(k_tile, qt_part) * scale
 
 
 def mask_t(scores, key_start, query_start, span):
     key_pos = key_start + lax.broadcasted_iota(jnp.int32, scores.shape, 0)
     query_pos = query_start + lax.broadcasted_iota(jnp.int32, scores.shape, 1) % span
     return jnp.where(key_pos <= query_pos, scores, NEG_FILL)
+
+
+def in_turn(count, multiply, weigh, collect):
+    for n in range(count + 2):
+        if n < count:
+            multiply(n)
+        if 1 <= n <= count:
+            weigh(n - 1)
+        if n >= 2:
+            collect(n - 2)
 
 
 def load_sorted(info_ref, src_ref, blocks, span):
@@ -60,9 +67,15 @@
         start = pl.multiple_of(j * PAIR, PAIR)
         k_tile = k_sorted[pl.ds(start, PAIR), :]
         v_tile = v_t[:, pl.ds(start, PAIR)]
-        for c in range(0, q_t.shape[1], COLS):
-            cols = slice(c, c + COLS)
-            scores = scores_t(k_tile, q_t[:, cols], scale)
+        parts = [slice(c, c + FORWARD_COLS) for c in range(0, q_t.shape[1], FORWARD_COLS)]
+        ready, weighted = {}, {}
+
+        def multiply(n):
+            ready[n] = dot(k_tile, q_t[:, parts[n]])
+
+        def weigh(n):
+            cols = parts[n]
+            scores = ready.pop(n) * scale
             if masked:
                 scores = mask_t(scores, start, query_block * span, span)
             old_top = top[:, cols]
@@ -71,7 +84,13 @@
             factor = jnp.exp2(old_top - new_top)
             top[:, cols] = new_top
             total[:, cols] = total[:, cols] * factor + jnp.sum(weights, axis=0, keepdims=True)
-            out_t[:, cols] = out_t[:, cols] * factor + dot(v_tile, weights.astype(BF16))
+            weighted[n] = (weights.astype(BF16), factor)
+
+        def collect(n):
+            weights, factor = weighted.pop(n)
+            out_t[:, parts[n]] = out_t[:, parts[n]] * factor + dot(v_tile, weights)
+
+        in_turn(len(parts), multiply, weigh, collect)
 
     last = query_block // 2
     pl.loop(0, last)(lambda j: step(j, False))
@@ -121,18 +140,26 @@
         k_tile = k_sorted[rows, :]
         v_tile = v_sorted[rows, :]
         kt_tile = k_t[:, rows]
-        all_w, all_d = [], []
-        for c in range(0, q_t.shape[1], COLS):
-            cols = slice(c, c + COLS)
-            scores = scores_t(k_tile, q_t[:, cols], scale)
+        parts = [slice(c, c + BACKWARD_COLS) for c in range(0, q_t.shape[1], BACKWARD_COLS)]
+        ready, all_w, all_d = {}, [], []
+
+        def multiply(n):
+            ready[n] = (dot(k_tile, q_t[:, parts[n]]), dot(v_tile, go_t[:, parts[n]]))
+
+        def weigh(n):
+            cols = parts[n]
+            products, dweights = ready.pop(n)
+            scores = products * scale
             if masked:
                 scores = mask_t(scores, start, query_block * span, span)
             weights = jnp.exp2(scores - lse_ref[0, 0, :, cols])
-            dweights = dot(v_tile, go_t[:, cols])
-            dscores = (weights * (dweights - delta[:, cols])).astype(BF16)
-            gq_t[:, cols] += dot(kt_tile, dscores)
             all_w.append(weights.astype(BF16))
-            all_d.append(dscores)
+            all_d.append((weights * (dweights - delta[:, cols])).astype(BF16))
+
+        def collect(n):
+            gq_t[:, parts[n]] += dot(kt_tile, all_d[n])
+
+        in_turn(len(parts), multiply, weigh, collect)
         gv[rows, :] += dot(jnp.concatenate(all_w, axis=1), go_s[...])
         gk[rows, :] += dot(jnp.concatenate(all_d, axis=1), q_s[...])
 
@@ -159,7 +186,7 @@
 
 def project(first, attended, weight, width):
     rows, depth = attended.shape
-    tile = 512
+    tile = 1024
     return pl.pallas_call(
         project_kernel,
         out_shape=jax.ShapeDtypeStruct((rows, width), BF16),
@@ -303,15 +330,26 @@
         grad_out, out_weight, (((1,), (1,)), ((), ())), preferred_element_type=F32
     ).astype(BF16)
 
+    q2, grad_heads = lax.optimization_barrier((q2, grad_heads))
     attended, att_t, lse = forward(info, q2, kv_all, span)
 
     early = jnp.where(me < (tp + 1) // 2, tp - 1, 0).astype(jnp.int32).reshape(1)
     first = project(early, attended, out_weight, chunk)
-    partial_out = project(jnp.zeros((1,), jnp.int32), attended, out_weight, model)
+    first, rest = lax.optimization_barrier((first, attended))
+    partial_out = project(jnp.zeros((1,), jnp.int32), rest, out_weight, model)
 
     def own_part(index):
         index = jnp.clip(index, 0, tp - 1)
         return lax.dynamic_slice_in_dim(partial_out, index * chunk, chunk, axis=1)
+
+    query_parts, kv_parts = [], []
+
+    def key_value_sum(now):
+        g = len(query_parts)
+        gq, gkv = backward(info, now, grad_heads, kv_all, att_t, lse, span, g)
+        query_parts.append(gq)
+        terms = gkv.reshape(ctx, 2, rows, hd)
+        kv_parts.append(lax.psum_scatter(terms, "ctx", scatter_dimension=0, tiled=False))
 
     right = left = first
     for k in range(tp - 1):
@@ -322,22 +360,16 @@
         if k < tp - 2:
             right = (own_part(tp - 2 - k + me).astype(F32) + from_left).astype(BF16)
             left = (own_part(k + 2 - tp + me).astype(F32) + from_right).astype(BF16)
+            right, left, q2 = lax.optimization_barrier((right, left, q2))
+            if len(query_parts) < kvl:
+                key_value_sum(q2)
+    while len(query_parts) < kvl:
+        key_value_sum(q2)
     layer_out = (own_part(me).astype(F32) + from_left + from_right).astype(BF16)
 
-    query_parts, kv_parts = [], []
-    for g in range(kvl):
-        gq, gkv = backward(info, q2, grad_heads, kv_all, att_t, lse, span, g)
-        query_parts.append(gq)
-        kv_parts.append(gkv)
     grad_queries = jnp.concatenate(query_parts, axis=1).reshape(rows, heads, hd)
-    terms = jnp.stack(kv_parts, axis=1).reshape(ctx, kvl, 2, rows, hd)
-    owned = lax.psum_scatter(terms, "ctx", scatter_dimension=0, tiled=False)
-    return (
-        layer_out,
-        grad_queries,
-        owned[:, 0].transpose(1, 0, 2),
-        owned[:, 1].transpose(1, 0, 2),
-    )
+    owned = jnp.stack(kv_parts, axis=2)
+    return (layer_out, grad_queries, owned[0], owned[1])
 
 
 def solution(mesh):

time: 223 us -> 196 us (0.88)
  Pallas kernels: 82.5 us -> 61.3 us
  waiting for transfers between devices: 73 us -> 62.9 us
  starting transfers between devices: 12.7 us -> 20.4 us
    all_gather x1, waiting for transfers between devices: 29.8 us -> 12.8 us  [local(): kv_all = lax.all_gather(kv, 'ctx', axis=0, tiled=False)]
    ppermute x3, waiting for transfers between devices: 0.01 us -> 14.6 us  [local(): from_left = lax.ppermute(right, 'tp', to_right).astype(F32)]
    pallas_call x1, Pallas kernels: 25.5 us -> 15.1 us  [forward(): pl.pallas_call(kernel, out_shape=(jax.ShapeDtypeStruct((rows, flat), BF16...]
    ppermute x3, waiting for transfers between devices: 16 us -> 5.87 us  [local(): from_right = lax.ppermute(left, 'tp', to_left).astype(F32)]
    convert_element_type x2 -> x0, other arithmetic: 7.4 us -> none  [local(): right = (own_part(tp - 2 - k + me).astype(F32) + from_left).astype(BF16)]
    ppermute x3, starting transfers between devices: 8.98 us -> 15.6 us  [local(): from_left = lax.ppermute(right, 'tp', to_right).astype(F32)]
    convert_element_type x1 -> x2, other arithmetic: 2.68 us -> 8.41 us  [local(): left = (own_part(k + 2 - tp + me).astype(F32) + from_right).astype(BF16)]
    pallas_call x2, Pallas kernels: 29.8 us -> 24.1 us  [backward(): pl.pallas_call(kernel, out_shape=(jax.ShapeDtypeStruct((rows, width), BF1...]
  transfers between devices with their start and end apart: 8 -> 9, of which waited for: 3 -> 6; matrix products, arithmetic and copies ran while one was open for 15% -> 14% of each run, Pallas kernels for 23% -> 21%
where the time goes in v2:
time: 196 us
  waiting for transfers between devices  62.9 us (32%)
  Pallas kernels  61.3 us (31%)
  starting transfers between devices  20.4 us (10%)
  matrix products  17 us (9%)
  other arithmetic  14.1 us (7%)
  between operations  13.8 us (7%)
  local copies, waits for them, and re-layouts  6.22 us (3%)
    reduce_scatter x2, waiting for transfers between devices, key_value_sum(): lax.psum_scatter(terms, 'ctx', scatter_dimension=0, tiled=False)  29.5 us
    pallas_call x2, Pallas kernels, backward(): pl.pallas_call(kernel, out_shape=(jax.ShapeDtypeStruct((rows, width), BF1...  24.1 us
    pallas_call x2, Pallas kernels, project(): pl.pallas_call(project_kernel, out_shape=jax.ShapeDtypeStruct((rows, widt...  22.1 us
    dot_general x1, matrix products, local(): lax.dot_general(grad_out, out_weight, (((1,), (1,)), ((), ())), preferred...  17 us
    ppermute x3, starting transfers between devices, local(): from_left = lax.ppermute(right, 'tp', to_right).astype(F32)  15.6 us
    pallas_call x1, Pallas kernels, forward(): pl.pallas_call(kernel, out_shape=(jax.ShapeDtypeStruct((rows, flat), BF16...  15.1 us
    ppermute x3, waiting for transfers between devices, local(): from_left = lax.ppermute(right, 'tp', to_right).astype(F32)  14.6 us
    all_gather x1, waiting for transfers between devices, local(): kv_all = lax.all_gather(kv, 'ctx', axis=0, tiled=False)  12.8 us
  transfers between devices with their start and end apart: 9, of which 6 were waited for; matrix products, arithmetic and copies ran while one was open for 14% of the time, Pallas kernels for 21%

profile of v2, /device:TPU:0, one launch (start us, length us, event | category | flops | bytes accessed | tf_op | source)
XLA Modules:
  0.0 195.7 jit_solution(8298144602969830036)
XLA Ops:
  7.2 1.4 maximum_bitcast_fusion.1
  9.4 1.5 copy.26
  10.9 17.0 %convolution_convert_fusion.go_ref = bf16[256,2048]{1,0:T(8,128)(2,1)} fusion(bf16[256,8192]{1,0:T(8,128)(2,1)} %param.11, bf16[2048,8192]{1,0:T(8,128)(2,1)} %w_ref.3), kind=kOutput, calls=%fused_computation | convolution fusion | flops 8590458880 | bytes 38797312 | tf_op jit(solution)/shard_map/dot_general | solution.py:329
  28.3 12.8 %all-gather.2.cloned.1.call-done.k_ref.v_ref = bf16[8,4,2,128,128]{4,3,2,1,0:T(8,128)(2,1)} async-done(((bf16[1,4,2,128,128]{4,3,2,1,0:T(8,128)(2,1)}), bf16[8,4,2,128,128]{4,3,2,1,0:T(8,128)(2,1)}) %all-gather.2.cloned.1.call-update) | async-done | bytes 2097168 | tf_op jit(solution)/shard_map/all_gather | solution.py:320
  41.1 15.1 %shard_map.93 = (bf16[256,2048]{1,0:T(8,128)(2,1)S(1)}, bf16[2,2,128,1024]{3,2,1,0:T(8,128)(2,1)S(1)}, f32[2,2,1,1024]{3,2,1,0:T(1,128)S(1)}) custom-call(s32[18]{0:T(128)S(1)} %pad_add_fusion.info_ref, bf16[256,2048]{1,0:T(8,128)(2,1)S(1)} %bitcast.24, bf16[8,4,2,128,128]{4,3,2,1,0:T(8,128)(2,1)} %all-gather.2.cloned.1.call-done.k_ref.v_ref, ...), custom_call_target="tpu_custom_call" | custom-call | flops 4294967296 | bytes 2097152 | tf_op jit(solution)/shard_map/pallas_call | solution.py:218
  57.2 4.8 %shard_map.94 = bf16[256,2048]{1,0:T(8,128)(2,1)S(1)} custom-call(s32[1]{0:T(128)} %bitcast.info_ref, bf16[256,2048]{1,0:T(8,128)(2,1)S(1)} %get-tuple-element.23.a_ref, bf16[2048,8192]{1,0:T(8,128)(2,1)} %w_ref.3), custom_call_target="tpu_custom_call" | custom-call | flops 2147483648 | bytes 8388608 | tf_op jit(solution)/shard_map/pallas_call | solution.py:190
  62.0 1.7 collective-permute-start.1
  63.7 4.3 %collective-permute-start = (bf16[256,2048]{1,0:T(8,128)(2,1)S(1)}, bf16[256,2048]{1,0:T(8,128)(2,1)}, u32[]{:S(2)}, u32[]{:S(2)}) collective-permute-start(bf16[256,2048]{1,0:T(8,128)(2,1)S(1)} %shard_map.94), channel_id=1, source_target_pairs={{0,1},{4,5},{8,9},{12,13},{16,17},{20,21},{24,25},{28,29}} | collective-permute-start | bytes 3145736 | tf_op jit(solution)/shard_map/ppermute | solution.py:358
  68.1 17.3 %shard_map.95 = bf16[256,8192]{1,0:T(8,128)(2,1)} custom-call(s32[1]{0:T(128)} %constant.15.clone.1.info_ref, bf16[256,2048]{1,0:T(8,128)(2,1)S(1)} %get-tuple-element.23.a_ref, bf16[2048,8192]{1,0:T(8,128)(2,1)} %w_ref.3), custom_call_target="tpu_custom_call" | custom-call | flops 8589934592 | bytes 33554432 | tf_op jit(solution)/shard_map/pallas_call | solution.py:190
  85.4 4.6 %collective-permute-done = bf16[256,2048]{1,0:T(8,128)(2,1)} collective-permute-done((bf16[256,2048]{1,0:T(8,128)(2,1)S(1)}, bf16[256,2048]{1,0:T(8,128)(2,1)}, u32[]{:S(2)}, u32[]{:S(2)}) %collective-permute-start) | collective-permute-done | bytes 1048608 | tf_op jit(solution)/shard_map/ppermute | solution.py:358
  90.0 4.0 %add_convert_fusion.3 = (bf16[256,2048]{1,0:T(8,128)(2,1)}, bf16[256,2048]{1,0:T(8,128)(2,1)S(1)}) fusion(bf16[256,2048]{1,0:T(8,128)(2,1)} %collective-permute-done.1, bf16[256,8192]{1,0:T(8,128)(2,1)} %shard_map.95, s32[]{:T(128)S(6)} %select_n.42, bf16[256,2048]{1,0:T(8,128)(2,1)} %collective-permute-done, s32[]{:T(128)S(6)} %select_n.41), kind=kLoop, calls=%fused_computation.4 | loop fusion | flops 4194304 | bytes 6291464 | tf_op jit(solution)/shard_map/convert_element_type | solution.py:362
  93.9 1.6 collective-permute-start.3
  95.6 5.1 %collective-permute-start.2 = (bf16[256,2048]{1,0:T(8,128)(2,1)S(1)}, bf16[256,2048]{1,0:T(8,128)(2,1)}, u32[]{:S(2)}, u32[]{:S(2)}) collective-permute-start(bf16[256,2048]{1,0:T(8,128)(2,1)S(1)} %get-tuple-element.25), channel_id=1, source_target_pairs={{0,1},{1,2},{4,5},{5,6},{8,9},{9,10},{12,13},{13,14},{16,17},{17,1... | collective-permute-start | bytes 3145736 | tf_op jit(solution)/shard_map/ppermute | solution.py:358
  100.7 12.1 %shard_map.96 = (bf16[256,1024]{1,0:T(8,128)(2,1)S(1)}, bf16[8,2,2,128,128]{4,3,2,1,0:T(8,128)(2,1)}) custom-call(s32[18]{0:T(128)S(1)} %pad_add_fusion.info_ref, bf16[256,2048]{1,0:T(8,128)(2,1)S(1)} %bitcast.25, bf16[256,2048]{1,0:T(8,128)(2,1)S(1)} %copy-done.1, bf16[8,4,2,128,128]{4,3,2,1,0:T(8,128)(2,1)} %all-gather.2.cloned.1.call-done.k_ref.v_ref, ...), custom_call_target="tpu_custom_call" | custom-call | flops 5368709120 | bytes 2097152 | tf_op jit(solution)/shard_map/pallas_call | solution.py:265
  112.9 8.8 %collective-permute-done.2 = bf16[256,2048]{1,0:T(8,128)(2,1)} collective-permute-done((bf16[256,2048]{1,0:T(8,128)(2,1)S(1)}, bf16[256,2048]{1,0:T(8,128)(2,1)}, u32[]{:S(2)}, u32[]{:S(2)}) %collective-permute-start.2) | collective-permute-done | bytes 1048608 | tf_op jit(solution)/shard_map/ppermute | solution.py:358
  121.7 4.5 %add_convert_fusion.1 = (bf16[256,2048]{1,0:T(8,128)(2,1)}, bf16[256,2048]{1,0:T(8,128)(2,1)}) fusion(bf16[256,2048]{1,0:T(8,128)(2,1)} %collective-permute-done.3, bf16[256,8192]{1,0:T(8,128)(2,1)} %shard_map.95, s32[]{:T(128)S(6)} %select_n.43, bf16[256,2048]{1,0:T(8,128)(2,1)} %collective-permute-done.2, s32[]{:T(128)S(6)} %select_n.40), kind=kLoop, calls=%fused_computation.2 | loop fusion | flops 4194304 | bytes 6291464 | tf_op jit(solution)/shard_map/convert_element_type | solution.py:362
  126.2 1.3 collective-permute-start.5
  127.5 6.1 %collective-permute-start.4 = (bf16[256,2048]{1,0:T(8,128)(2,1)}, bf16[256,2048]{1,0:T(8,128)(2,1)}, u32[]{:S(2)}, u32[]{:S(2)}) collective-permute-start(bf16[256,2048]{1,0:T(8,128)(2,1)} %get-tuple-element.28), channel_id=1, source_target_pairs={{0,1},{1,2},{2,3},{4,5},{5,6},{6,7},{8,9},{9,10},{10,11},{12,13},{... | collective-permute-start | bytes 3145736 | tf_op jit(solution)/shard_map/ppermute | solution.py:358
  133.6 12.0 %shard_map.97 = (bf16[256,1024]{1,0:T(8,128)(2,1)S(1)}, bf16[8,2,2,128,128]{4,3,2,1,0:T(8,128)(2,1)}) custom-call(s32[18]{0:T(128)S(1)} %pad_add_fusion.info_ref, bf16[256,2048]{1,0:T(8,128)(2,1)S(1)} %bitcast.26, bf16[256,2048]{1,0:T(8,128)(2,1)S(1)} %copy-done.2, bf16[8,4,2,128,128]{4,3,2,1,0:T(8,128)(2,1)} %all-gather.2.cloned.1.call-done.k_ref.v_ref, ...), custom_call_target="tpu_custom_call" | custom-call | flops 5368709120 | bytes 2097152 | tf_op jit(solution)/shard_map/pallas_call | solution.py:265
  145.7 1.2 copy.24
  146.9 5.9 %collective-permute-done.5 = bf16[256,2048]{1,0:T(8,128)(2,1)S(1)} collective-permute-done((bf16[256,2048]{1,0:T(8,128)(2,1)}, bf16[256,2048]{1,0:T(8,128)(2,1)S(1)}, u32[]{:S(2)}, u32[]{:S(2)}) %collective-permute-start.5) | collective-permute-done | bytes 1048608 | tf_op jit(solution)/shard_map/ppermute | solution.py:359
  152.8 1.3 collective-permute-done.4
  154.1 3.1 %add_convert_fusion = bf16[256,2048]{1,0:T(8,128)(2,1)} fusion(bf16[256,2048]{1,0:T(8,128)(2,1)S(1)} %collective-permute-done.5, bf16[256,2048]{1,0:T(8,128)(2,1)} %collective-permute-done.4, bf16[256,8192]{1,0:T(8,128)(2,1)} %shard_map.95, s32[]{:T(128)S(6)} %select_n.39), kind=kLoop, calls=%fused_computation.1 | loop fusion | flops 3145728 | bytes 4194308 | tf_op jit(solution)/shard_map/convert_element_type | solution.py:368
  157.1 29.5 %reduce-scatter.5.cloned.1.call-done = bf16[1,2,256,128]{3,2,1,0:T(8,128)(2,1)} async-done(((bf16[8,2,256,128]{3,2,1,0:T(8,128)(2,1)}), bf16[1,2,256,128]{3,2,1,0:T(8,128)(2,1)}) %reduce-scatter.5.cloned.1.call-update) | async-done | bytes 131088 | tf_op jit(solution)/shard_map/reduce_scatter | solution.py:352
  (27 shorter events, 4.9 us)
Async XLA Ops:
  7.2 33.9 %all-gather.2.cloned.1.call-start = ((), (), s32[]{:S(2)}) async-start(), calls=%async_computation.2 | async-start | bytes 2359296 | tf_op jit(solution)/shard_map/all_gather | solution.py:320
  9.3 147.8 %reduce-scatter.3.cloned.1.call-start = ((), (), s32[]{:S(2)}) async-start(), calls=%async_computation.3 | async-start | bytes 1179648 | tf_op jit(solution)/shard_map/reduce_scatter | solution.py:352
  10.9 17.0 %copy-start.3 = (s32[2048]{0:T(1024)S(1)}, s32[2048]{0:T(1024)}, u32[]{:S(2)}) copy-start(s32[2048]{0:T(1024)} %param.9) | copy-start | bytes 24580
  56.2 1.0 copy-start
  62.0 23.4 %collective-permute-start.1 = (bf16[256,2048]{1,0:T(8,128)(2,1)S(1)}, bf16[256,2048]{1,0:T(8,128)(2,1)}, u32[]{:S(2)}, u32[]{:S(2)}) collective-permute-start(bf16[256,2048]{1,0:T(8,128)(2,1)S(1)} %shard_map.94), channel_id=1, source_target_pairs={{3,2},{7,6},{11,10},{15,14},{19,18},{23,22},{27,26},{31,30}} | collective-permute-start | bytes 3145736 | tf_op jit(solution)/shard_map/ppermute | solution.py:359
  63.7 26.2 %collective-permute-start = (bf16[256,2048]{1,0:T(8,128)(2,1)S(1)}, bf16[256,2048]{1,0:T(8,128)(2,1)}, u32[]{:S(2)}, u32[]{:S(2)}) collective-permute-start(bf16[256,2048]{1,0:T(8,128)(2,1)S(1)} %shard_map.94), channel_id=1, source_target_pairs={{0,1},{4,5},{8,9},{12,13},{16,17},{20,21},{24,25},{28,29}} | collective-permute-start | bytes 3145736 | tf_op jit(solution)/shard_map/ppermute | solution.py:358
  85.4 15.3 %copy-start.1 = (bf16[256,2048]{1,0:T(8,128)(2,1)S(1)}, bf16[256,2048]{1,0:T(8,128)(2,1)}, u32[]{:S(2)}) copy-start(bf16[256,2048]{1,0:T(8,128)(2,1)} %convolution_convert_fusion.go_ref) | copy-start | bytes 3145732
  93.9 19.0 %collective-permute-start.3 = (bf16[256,2048]{1,0:T(8,128)(2,1)}, bf16[256,2048]{1,0:T(8,128)(2,1)}, u32[]{:S(2)}, u32[]{:S(2)}) collective-permute-start(bf16[256,2048]{1,0:T(8,128)(2,1)} %get-tuple-element.26), channel_id=1, source_target_pairs={{3,2},{2,1},{7,6},{6,5},{11,10},{10,9},{15,14},{14,13},{19,18},{18... | collective-permute-start | bytes 3145736 | tf_op jit(solution)/shard_map/ppermute | solution.py:359
  95.6 26.2 %collective-permute-start.2 = (bf16[256,2048]{1,0:T(8,128)(2,1)S(1)}, bf16[256,2048]{1,0:T(8,128)(2,1)}, u32[]{:S(2)}, u32[]{:S(2)}) collective-permute-start(bf16[256,2048]{1,0:T(8,128)(2,1)S(1)} %get-tuple-element.25), channel_id=1, source_target_pairs={{0,1},{1,2},{4,5},{5,6},{8,9},{9,10},{12,13},{13,14},{16,17},{17,1... | collective-permute-start | bytes 3145736 | tf_op jit(solution)/shard_map/ppermute | solution.py:358
  112.8 73.7 %reduce-scatter.5.cloned.1.call-start = ((), (), s32[]{:S(2)}) async-start(), calls=%async_computation.4 | async-start | bytes 1179648 | tf_op jit(solution)/shard_map/reduce_scatter | solution.py:352
  112.9 20.7 %copy-start.2 = (bf16[256,2048]{1,0:T(8,128)(2,1)S(1)}, bf16[256,2048]{1,0:T(8,128)(2,1)}, u32[]{:S(2)}) copy-start(bf16[256,2048]{1,0:T(8,128)(2,1)} %convolution_convert_fusion.go_ref) | copy-start | bytes 3145732
  126.2 26.6 %collective-permute-start.5 = (bf16[256,2048]{1,0:T(8,128)(2,1)}, bf16[256,2048]{1,0:T(8,128)(2,1)S(1)}, u32[]{:S(2)}, u32[]{:S(2)}) collective-permute-start(bf16[256,2048]{1,0:T(8,128)(2,1)} %get-tuple-element.29), channel_id=1, source_target_pairs={{3,2},{2,1},{1,0},{7,6},{6,5},{5,4},{11,10},{10,9},{9,8},{15,14},{... | collective-permute-start | bytes 3145736 | tf_op jit(solution)/shard_map/ppermute | solution.py:359
  127.5 26.6 %collective-permute-start.4 = (bf16[256,2048]{1,0:T(8,128)(2,1)}, bf16[256,2048]{1,0:T(8,128)(2,1)}, u32[]{:S(2)}, u32[]{:S(2)}) collective-permute-start(bf16[256,2048]{1,0:T(8,128)(2,1)} %get-tuple-element.28), channel_id=1, source_target_pairs={{0,1},{1,2},{2,3},{4,5},{5,6},{6,7},{8,9},{9,10},{10,11},{12,13},{... | collective-permute-start | bytes 3145736 | tf_op jit(solution)/shard_map/ppermute | solution.py:358
Sparse Core Ops, SparseCore 0:
  10.5 30.5 all-gather.1
  113.0 34.3 reduce-scatter.2
  150.5 35.9 reduce-scatter.4

commit v3 on v2

--- a/solution.py
+++ b/solution.py
@@ -342,15 +342,13 @@
         index = jnp.clip(index, 0, tp - 1)
         return lax.dynamic_slice_in_dim(partial_out, index * chunk, chunk, axis=1)
 
-    query_parts, kv_parts = [], []
-
-    def key_value_sum(now):
-        g = len(query_parts)
-        gq, gkv = backward(info, now, grad_heads, kv_all, att_t, lse, span, g)
-        query_parts.append(gq)
-        terms = gkv.reshape(ctx, 2, rows, hd)
-        kv_parts.append(lax.psum_scatter(terms, "ctx", scatter_dimension=0, tiled=False))
-
+    def gradients(now):
+        parts = [backward(info, now, grad_heads, kv_all, att_t, lse, span, g) for g in range(kvl)]
+        queries_part = jnp.concatenate([part[0] for part in parts], axis=1)
+        terms = jnp.stack([part[1] for part in parts], axis=1).reshape(ctx, kvl, 2, rows, hd)
+        return queries_part, lax.psum_scatter(terms, "ctx", scatter_dimension=0, tiled=False)
+
+    grads = None
     right = left = first
     for k in range(tp - 1):
         to_right = [(z, z + 1) for z in range(tp - 1) if z <= k]
@@ -361,14 +359,14 @@
             right = (own_part(tp - 2 - k + me).astype(F32) + from_left).astype(BF16)
             left = (own_part(k + 2 - tp + me).astype(F32) + from_right).astype(BF16)
             right, left, q2 = lax.optimization_barrier((right, left, q2))
-            if len(query_parts) < kvl:
-                key_value_sum(q2)
-    while len(query_parts) < kvl:
-        key_value_sum(q2)
+            if grads is None:
+                grads = gradients(q2)
+    if grads is None:
+        grads = gradients(q2)
     layer_out = (own_part(me).astype(F32) + from_left + from_right).astype(BF16)
 
-    grad_queries = jnp.concatenate(query_parts, axis=1).reshape(rows, heads, hd)
-    owned = jnp.stack(kv_parts, axis=2)
+    grad_queries = grads[0].reshape(rows, heads, hd)
+    owned = grads[1].transpose(1, 2, 0, 3)
     return (layer_out, grad_queries, owned[0], owned[1])
 
 

time: 196 us -> 174 us (0.89)
  waiting for transfers between devices: 62.9 us -> 42.9 us
  Pallas kernels: 61.3 us -> 59.2 us
    reduce_scatter x2 -> x1, waiting for transfers between devices: 29.5 us -> 5.07 us  [gradients(): lax.psum_scatter(terms, 'ctx', scatter_dimension=0, tiled=False)]
    ppermute x3, waiting for transfers between devices: 5.87 us -> 19.1 us  [local(): from_right = lax.ppermute(left, 'tp', to_left).astype(F32)]
    ppermute x3, waiting for transfers between devices: 14.6 us -> 5.8 us  [local(): from_left = lax.ppermute(right, 'tp', to_right).astype(F32)]
    pallas_call x2, Pallas kernels: 24.1 us -> 22.1 us  [backward(): pl.pallas_call(kernel, out_shape=(jax.ShapeDtypeStruct((rows, width), BF1...]
    unnamed x12 -> x10, local copies, waits for them, and re-layouts: 5.29 us -> 5.27 us
  transfers between devices with their start and end apart: 9 -> 8, of which waited for: 6 -> 5; matrix products, arithmetic and copies ran while one was open for 14% -> 17% of each run, Pallas kernels for 21% -> 23%
where the time goes in v3:
time: 174 us
  Pallas kernels  59.2 us (34%)
  waiting for transfers between devices  42.9 us (25%)
  starting transfers between devices  18.9 us (11%)
  matrix products  16.9 us (10%)
  other arithmetic  14.3 us (8%)
  between operations  14.2 us (8%)
  local copies, waits for them, and re-layouts  7.19 us (4%)
    pallas_call x2, Pallas kernels, backward(): pl.pallas_call(kernel, out_shape=(jax.ShapeDtypeStruct((rows, width), BF1...  22.1 us
    pallas_call x2, Pallas kernels, project(): pl.pallas_call(project_kernel, out_shape=jax.ShapeDtypeStruct((rows, widt...  22 us
    ppermute x3, waiting for transfers between devices, local(): from_right = lax.ppermute(left, 'tp', to_left).astype(F32)  19.1 us
    dot_general x1, matrix products, local(): lax.dot_general(grad_out, out_weight, (((1,), (1,)), ((), ())), preferred...  16.9 us
    pallas_call x1, Pallas kernels, forward(): pl.pallas_call(kernel, out_shape=(jax.ShapeDtypeStruct((rows, flat), BF16...  15.1 us
    ppermute x3, starting transfers between devices, local(): from_left = lax.ppermute(right, 'tp', to_right).astype(F32)  14.2 us
    all_gather x1, waiting for transfers between devices, local(): kv_all = lax.all_gather(kv, 'ctx', axis=0, tiled=False)  12.9 us
    convert_element_type x2, other arithmetic, local(): left = (own_part(k + 2 - tp + me).astype(F32) + from_right).astype(BF16)  8.39 us
  transfers between devices with their start and end apart: 8, of which 5 were waited for; matrix products, arithmetic and copies ran while one was open for 17% of the time, Pallas kernels for 23%

profile of v3, /device:TPU:0, one launch (start us, length us, event | category | flops | bytes accessed | tf_op | source)
XLA Modules:
  0.0 173.6 jit_solution(7888423955139967950)
XLA Ops:
  7.2 1.4 maximum_bitcast_fusion.1
  9.4 1.5 copy.32
  10.9 16.9 %convolution_convert_fusion.go_ref = bf16[256,2048]{1,0:T(8,128)(2,1)} fusion(bf16[256,8192]{1,0:T(8,128)(2,1)} %param.11, bf16[2048,8192]{1,0:T(8,128)(2,1)} %w_ref.3), kind=kOutput, calls=%fused_computation | convolution fusion | flops 8590458880 | bytes 38797312 | tf_op jit(solution)/shard_map/dot_general | solution.py:329
  28.2 12.9 %all-gather.2.cloned.1.call-done.k_ref.v_ref = bf16[8,4,2,128,128]{4,3,2,1,0:T(8,128)(2,1)} async-done(((bf16[1,4,2,128,128]{4,3,2,1,0:T(8,128)(2,1)}), bf16[8,4,2,128,128]{4,3,2,1,0:T(8,128)(2,1)}) %all-gather.2.cloned.1.call-update) | async-done | bytes 2097168 | tf_op jit(solution)/shard_map/all_gather | solution.py:320
  41.1 15.1 %shard_map.93 = (bf16[256,2048]{1,0:T(8,128)(2,1)S(1)}, bf16[2,2,128,1024]{3,2,1,0:T(8,128)(2,1)S(1)}, f32[2,2,1,1024]{3,2,1,0:T(1,128)S(1)}) custom-call(s32[18]{0:T(128)S(1)} %pad_add_fusion.info_ref, bf16[256,2048]{1,0:T(8,128)(2,1)S(1)} %bitcast.29, bf16[8,4,2,128,128]{4,3,2,1,0:T(8,128)(2,1)} %all-gather.2.cloned.1.call-done.k_ref.v_ref, ...), custom_call_target="tpu_custom_call" | custom-call | flops 4294967296 | bytes 2097152 | tf_op jit(solution)/shard_map/pallas_call | solution.py:218
  57.2 4.8 %shard_map.94 = bf16[256,2048]{1,0:T(8,128)(2,1)S(1)} custom-call(s32[1]{0:T(128)} %bitcast.info_ref, bf16[256,2048]{1,0:T(8,128)(2,1)S(1)} %get-tuple-element.22.a_ref, bf16[2048,8192]{1,0:T(8,128)(2,1)} %w_ref.3), custom_call_target="tpu_custom_call" | custom-call | flops 2147483648 | bytes 8388608 | tf_op jit(solution)/shard_map/pallas_call | solution.py:190
  62.0 1.7 collective-permute-start.1
  63.7 4.4 %collective-permute-start = (bf16[256,2048]{1,0:T(8,128)(2,1)S(1)}, bf16[256,2048]{1,0:T(8,128)(2,1)}, u32[]{:S(2)}, u32[]{:S(2)}) collective-permute-start(bf16[256,2048]{1,0:T(8,128)(2,1)S(1)} %shard_map.94), channel_id=1, source_target_pairs={{0,1},{4,5},{8,9},{12,13},{16,17},{20,21},{24,25},{28,29}} | collective-permute-start | bytes 3145736 | tf_op jit(solution)/shard_map/ppermute | solution.py:356
  68.1 17.3 %shard_map.95 = bf16[256,8192]{1,0:T(8,128)(2,1)} custom-call(s32[1]{0:T(128)} %constant.15.clone.1.info_ref, bf16[256,2048]{1,0:T(8,128)(2,1)S(1)} %get-tuple-element.22.a_ref, bf16[2048,8192]{1,0:T(8,128)(2,1)} %w_ref.3), custom_call_target="tpu_custom_call" | custom-call | flops 8589934592 | bytes 33554432 | tf_op jit(solution)/shard_map/pallas_call | solution.py:190
  85.4 4.5 %collective-permute-done = bf16[256,2048]{1,0:T(8,128)(2,1)} collective-permute-done((bf16[256,2048]{1,0:T(8,128)(2,1)S(1)}, bf16[256,2048]{1,0:T(8,128)(2,1)}, u32[]{:S(2)}, u32[]{:S(2)}) %collective-permute-start) | collective-permute-done | bytes 1048608 | tf_op jit(solution)/shard_map/ppermute | solution.py:356
  89.9 4.0 %add_convert_fusion.3 = (bf16[256,2048]{1,0:T(8,128)(2,1)}, bf16[256,2048]{1,0:T(8,128)(2,1)S(1)}) fusion(bf16[256,2048]{1,0:T(8,128)(2,1)} %collective-permute-done.1, bf16[256,8192]{1,0:T(8,128)(2,1)} %shard_map.95, s32[]{:T(128)S(6)} %select_n.42, bf16[256,2048]{1,0:T(8,128)(2,1)} %collective-permute-done, s32[]{:T(128)S(6)} %select_n.41), kind=kLoop, calls=%fused_computation.5 | loop fusion | flops 4194304 | bytes 6291464 | tf_op jit(solution)/shard_map/convert_element_type | solution.py:360
  93.8 1.7 collective-permute-start.3
  95.5 5.2 %collective-permute-start.2 = (bf16[256,2048]{1,0:T(8,128)(2,1)S(1)}, bf16[256,2048]{1,0:T(8,128)(2,1)}, u32[]{:S(2)}, u32[]{:S(2)}) collective-permute-start(bf16[256,2048]{1,0:T(8,128)(2,1)S(1)} %get-tuple-element.24), channel_id=1, source_target_pairs={{0,1},{1,2},{4,5},{5,6},{8,9},{9,10},{12,13},{13,14},{16,17},{17,1... | collective-permute-start | bytes 3145736 | tf_op jit(solution)/shard_map/ppermute | solution.py:356
  100.7 11.1 %shard_map.97 = (bf16[256,1024]{1,0:T(8,128)(2,1)S(1)}, bf16[8,2,2,128,128]{4,3,2,1,0:T(8,128)(2,1)S(1)}) custom-call(s32[18]{0:T(128)S(1)} %pad_add_fusion.info_ref, bf16[256,2048]{1,0:T(8,128)(2,1)S(1)} %bitcast.30, bf16[256,2048]{1,0:T(8,128)(2,1)S(1)} %copy-done.1, bf16[8,4,2,128,128]{4,3,2,1,0:T(8,128)(2,1)} %all-gather.2.cloned.1.call-done.k_ref.v_ref, ...), custom_call_target="tpu_custom_call" | custom-call | flops 5368709120 | bytes 2097152 | tf_op jit(solution)/shard_map/pallas_call | solution.py:265
  111.8 11.1 %shard_map.96 = (bf16[256,1024]{1,0:T(8,128)(2,1)S(1)}, bf16[8,2,2,128,128]{4,3,2,1,0:T(8,128)(2,1)S(1)}) custom-call(s32[18]{0:T(128)S(1)} %pad_add_fusion.info_ref, bf16[256,2048]{1,0:T(8,128)(2,1)S(1)} %bitcast.31, bf16[256,2048]{1,0:T(8,128)(2,1)S(1)} %copy-done.1, bf16[8,4,2,128,128]{4,3,2,1,0:T(8,128)(2,1)} %all-gather.2.cloned.1.call-done.k_ref.v_ref, ...), custom_call_target="tpu_custom_call" | custom-call | flops 5368709120 | bytes 2097152 | tf_op jit(solution)/shard_map/pallas_call | solution.py:265
  122.8 1.5 pad_maximum_fusion
  124.4 4.4 %add_convert_fusion.1 = (bf16[256,2048]{1,0:T(8,128)(2,1)}, bf16[256,2048]{1,0:T(8,128)(2,1)}) fusion(bf16[256,2048]{1,0:T(8,128)(2,1)} %collective-permute-done.3, bf16[256,8192]{1,0:T(8,128)(2,1)} %shard_map.95, s32[]{:T(128)S(6)} %select_n.43, bf16[256,2048]{1,0:T(8,128)(2,1)} %collective-permute-done.2, s32[]{:T(128)S(6)} %select_n.40), kind=kLoop, calls=%fused_computation.3 | loop fusion | flops 4194304 | bytes 6291464 | tf_op jit(solution)/shard_map/convert_element_type | solution.py:360
  128.8 1.3 collective-permute-start.5
  130.1 4.6 %collective-permute-start.4 = (bf16[256,2048]{1,0:T(8,128)(2,1)}, bf16[256,2048]{1,0:T(8,128)(2,1)S(1)}, u32[]{:S(2)}, u32[]{:S(2)}) collective-permute-start(bf16[256,2048]{1,0:T(8,128)(2,1)} %get-tuple-element.27), channel_id=1, source_target_pairs={{0,1},{1,2},{2,3},{4,5},{5,6},{6,7},{8,9},{9,10},{10,11},{12,13},{... | collective-permute-start | bytes 3145736 | tf_op jit(solution)/shard_map/ppermute | solution.py:356
  134.8 1.2 copy.30
  136.0 19.1 %collective-permute-done.5 = bf16[256,2048]{1,0:T(8,128)(2,1)S(1)} collective-permute-done((bf16[256,2048]{1,0:T(8,128)(2,1)}, bf16[256,2048]{1,0:T(8,128)(2,1)S(1)}, u32[]{:S(2)}, u32[]{:S(2)}) %collective-permute-start.5) | collective-permute-done | bytes 1048608 | tf_op jit(solution)/shard_map/ppermute | solution.py:357
  155.1 1.3 collective-permute-done.4
  156.4 2.7 %add_convert_fusion = bf16[256,2048]{1,0:T(8,128)(2,1)} fusion(bf16[256,2048]{1,0:T(8,128)(2,1)S(1)} %collective-permute-done.5, bf16[256,2048]{1,0:T(8,128)(2,1)S(1)} %collective-permute-done.4, bf16[256,8192]{1,0:T(8,128)(2,1)} %shard_map.95, s32[]{:T(128)S(6)} %select_n.39), kind=kLoop, calls=%fused_computation.2 | loop fusion | flops 3145728 | bytes 4194308 | tf_op jit(solution)/shard_map/convert_element_type | solution.py:366
  159.1 5.1 %reduce-scatter.2.cloned.1.call-done = bf16[1,2,2,256,128]{4,3,2,1,0:T(8,128)(2,1)} async-done(((bf16[8,2,2,256,128]{4,3,2,1,0:T(8,128)(2,1)}), bf16[1,2,2,256,128]{4,3,2,1,0:T(8,128)(2,1)}) %reduce-scatter.2.cloned.1.call-update) | async-done | bytes 262160 | tf_op jit(solution)/shard_map/reduce_scatter | solution.py:349
  (23 shorter events, 4.9 us)
Async XLA Ops:
  7.2 33.9 %all-gather.2.cloned.1.call-start = ((), (), s32[]{:S(2)}) async-start(), calls=%async_computation.1 | async-start | bytes 2359296 | tf_op jit(solution)/shard_map/all_gather | solution.py:320
  9.3 154.9 %reduce-scatter.2.cloned.1.call-start = ((), (), s32[]{:S(2)}) async-start(), calls=%async_computation.2 | async-start | bytes 2359296 | tf_op jit(solution)/shard_map/reduce_scatter | solution.py:349
  10.9 16.9 %copy-start.2 = (s32[2048]{0:T(1024)S(1)}, s32[2048]{0:T(1024)}, u32[]{:S(2)}) copy-start(s32[2048]{0:T(1024)} %param.9) | copy-start | bytes 24580
  56.2 1.0 copy-start
  62.0 23.4 %collective-permute-start.1 = (bf16[256,2048]{1,0:T(8,128)(2,1)S(1)}, bf16[256,2048]{1,0:T(8,128)(2,1)}, u32[]{:S(2)}, u32[]{:S(2)}) collective-permute-start(bf16[256,2048]{1,0:T(8,128)(2,1)S(1)} %shard_map.94), channel_id=1, source_target_pairs={{3,2},{7,6},{11,10},{15,14},{19,18},{23,22},{27,26},{31,30}} | collective-permute-start | bytes 3145736 | tf_op jit(solution)/shard_map/ppermute | solution.py:357
  63.7 26.2 %collective-permute-start = (bf16[256,2048]{1,0:T(8,128)(2,1)S(1)}, bf16[256,2048]{1,0:T(8,128)(2,1)}, u32[]{:S(2)}, u32[]{:S(2)}) collective-permute-start(bf16[256,2048]{1,0:T(8,128)(2,1)S(1)} %shard_map.94), channel_id=1, source_target_pairs={{0,1},{4,5},{8,9},{12,13},{16,17},{20,21},{24,25},{28,29}} | collective-permute-start | bytes 3145736 | tf_op jit(solution)/shard_map/ppermute | solution.py:356
  85.4 15.3 %copy-start.1 = (bf16[256,2048]{1,0:T(8,128)(2,1)S(1)}, bf16[256,2048]{1,0:T(8,128)(2,1)}, u32[]{:S(2)}) copy-start(bf16[256,2048]{1,0:T(8,128)(2,1)} %convolution_convert_fusion.go_ref) | copy-start | bytes 3145732
  93.8 30.5 %collective-permute-start.3 = (bf16[256,2048]{1,0:T(8,128)(2,1)}, bf16[256,2048]{1,0:T(8,128)(2,1)}, u32[]{:S(2)}, u32[]{:S(2)}) collective-permute-start(bf16[256,2048]{1,0:T(8,128)(2,1)} %get-tuple-element.25), channel_id=1, source_target_pairs={{3,2},{2,1},{7,6},{6,5},{11,10},{10,9},{15,14},{14,13},{19,18},{18... | collective-permute-start | bytes 3145736 | tf_op jit(solution)/shard_map/ppermute | solution.py:357
  95.5 28.9 %collective-permute-start.2 = (bf16[256,2048]{1,0:T(8,128)(2,1)S(1)}, bf16[256,2048]{1,0:T(8,128)(2,1)}, u32[]{:S(2)}, u32[]{:S(2)}) collective-permute-start(bf16[256,2048]{1,0:T(8,128)(2,1)S(1)} %get-tuple-element.24), channel_id=1, source_target_pairs={{0,1},{1,2},{4,5},{5,6},{8,9},{9,10},{12,13},{13,14},{16,17},{17,1... | collective-permute-start | bytes 3145736 | tf_op jit(solution)/shard_map/ppermute | solution.py:356
  128.8 26.3 %collective-permute-start.5 = (bf16[256,2048]{1,0:T(8,128)(2,1)}, bf16[256,2048]{1,0:T(8,128)(2,1)S(1)}, u32[]{:S(2)}, u32[]{:S(2)}) collective-permute-start(bf16[256,2048]{1,0:T(8,128)(2,1)} %get-tuple-element.28), channel_id=1, source_target_pairs={{3,2},{2,1},{1,0},{7,6},{6,5},{5,4},{11,10},{10,9},{9,8},{15,14},{... | collective-permute-start | bytes 3145736 | tf_op jit(solution)/shard_map/ppermute | solution.py:357
  130.1 26.3 %collective-permute-start.4 = (bf16[256,2048]{1,0:T(8,128)(2,1)}, bf16[256,2048]{1,0:T(8,128)(2,1)S(1)}, u32[]{:S(2)}, u32[]{:S(2)}) collective-permute-start(bf16[256,2048]{1,0:T(8,128)(2,1)} %get-tuple-element.27), channel_id=1, source_target_pairs={{0,1},{1,2},{2,3},{4,5},{5,6},{6,7},{8,9},{9,10},{10,11},{12,13},{... | collective-permute-start | bytes 3145736 | tf_op jit(solution)/shard_map/ppermute | solution.py:356
Sparse Core Ops, SparseCore 0:
  10.5 30.5 all-gather.1
  124.5 39.6 reduce-scatter.1

commit v4 on v3

--- a/solution.py
+++ b/solution.py
@@ -100,15 +100,15 @@
     inverse = 1.0 / total[...]
     for h in range(heads):
         cols = slice(h * span, (h + 1) * span)
-        part = out_t[:, cols] * inverse[:, cols]
-        att_t_ref[0, 0, :, cols] = part.astype(BF16)
-        att_ref[:, cols] = part.T.astype(BF16)
+        part = (out_t[:, cols] * inverse[:, cols]).astype(BF16)
+        att_t_ref[0, 0, :, cols] = part
+        att_ref[:, cols] = part.T
 
 
 def backward_kernel(blocks, span, scale, out_scale, info_ref, q_ref, go_ref, k_ref, v_ref, att_t_ref,
                     lse_ref, gq_ref, gkv_ref, k_sorted, v_sorted, k_t, q_s, q_t, go_s, go_t, gq_t,
                     delta, gk, gv):
-    half = pl.program_id(0)
+    half = pl.program_id(1)
     heads = q_ref.shape[1] // span
     query_block = info_ref[blocks + half]
 
@@ -169,15 +169,15 @@
 
     for h in range(heads):
         part = slice(h * span, (h + 1) * span)
-        gq_ref[:, part] = (gq_t[:, part] * out_scale).T.astype(BF16)
+        gq_ref[:, part] = (gq_t[:, part] * out_scale).astype(BF16).T
 
     @pl.when(half == 1)
     def _():
         for j in range(blocks):
             stored = info_ref[j]
             part = slice(j * span, (j + 1) * span)
-            gkv_ref[stored // 2, 0, stored % 2] = (gk[part, :] * out_scale).astype(BF16)
-            gkv_ref[stored // 2, 1, stored % 2] = gv[part, :].astype(BF16)
+            gkv_ref[stored // 2, 0, 0, stored % 2] = (gk[part, :] * out_scale).astype(BF16)
+            gkv_ref[stored // 2, 0, 1, stored % 2] = gv[part, :].astype(BF16)
 
 
 def project_kernel(info_ref, a_ref, w_ref, o_ref):
@@ -186,7 +186,7 @@
 
 def project(first, attended, weight, width):
     rows, depth = attended.shape
-    tile = 1024
+    tile = min(1024, width)
     return pl.pallas_call(
         project_kernel,
         out_shape=jax.ShapeDtypeStruct((rows, width), BF16),
@@ -251,7 +251,7 @@
     )(info, q2, kv_all, kv_all)
 
 
-def backward(info, q2, go2, kv_all, att_t, lse, span, g):
+def backward(info, q2, go2, kv_all, att_t, lse, span):
     rows, flat = q2.shape
     ctx, kv2, _, _, hd = kv_all.shape
     kvl = kv2 // 2
@@ -261,27 +261,27 @@
     kernel = functools.partial(
         backward_kernel, blocks, span, LOG2E / math.sqrt(hd), 1.0 / math.sqrt(hd)
     )
-    work = rows * seq * width // 2
+    work = rows * seq * flat // 2
     return pl.pallas_call(
         kernel,
         out_shape=(
-            jax.ShapeDtypeStruct((rows, width), BF16),
-            jax.ShapeDtypeStruct((ctx, 2, 2, span, hd), BF16),
+            jax.ShapeDtypeStruct((rows, flat), BF16),
+            jax.ShapeDtypeStruct((ctx, kvl, 2, 2, span, hd), BF16),
         ),
         grid_spec=pltpu.PrefetchScalarGridSpec(
             num_scalar_prefetch=1,
-            grid=(2,),
+            grid=(kvl, 2),
             in_specs=[
-                pl.BlockSpec((span, width), lambda i, info: (i, g)),
-                pl.BlockSpec((span, width), lambda i, info: (i, g)),
-                pl.BlockSpec((ctx, 1, 2, span, hd), lambda i, info: (0, g, 0, 0, 0)),
-                pl.BlockSpec((ctx, 1, 2, span, hd), lambda i, info: (0, kvl + g, 0, 0, 0)),
-                pl.BlockSpec((1, 1, hd, width), lambda i, info: (g, i, 0, 0)),
-                pl.BlockSpec((1, 1, 1, width), lambda i, info: (g, i, 0, 0)),
+                pl.BlockSpec((span, width), lambda g, i, info: (i, g)),
+                pl.BlockSpec((span, width), lambda g, i, info: (i, g)),
+                pl.BlockSpec((ctx, 1, 2, span, hd), lambda g, i, info: (0, g, 0, 0, 0)),
+                pl.BlockSpec((ctx, 1, 2, span, hd), lambda g, i, info: (0, kvl + g, 0, 0, 0)),
+                pl.BlockSpec((1, 1, hd, width), lambda g, i, info: (g, i, 0, 0)),
+                pl.BlockSpec((1, 1, 1, width), lambda g, i, info: (g, i, 0, 0)),
             ],
             out_specs=(
-                pl.BlockSpec((span, width), lambda i, info: (i, 0)),
-                pl.BlockSpec((ctx, 2, 2, span, hd), lambda i, info: (0, 0, 0, 0, 0)),
+                pl.BlockSpec((span, width), lambda g, i, info: (i, g)),
+                pl.BlockSpec((ctx, 1, 2, 2, span, hd), lambda g, i, info: (0, g, 0, 0, 0, 0)),
             ),
             scratch_shapes=[
                 pltpu.VMEM((seq, hd), BF16),
@@ -343,9 +343,8 @@
         return lax.dynamic_slice_in_dim(partial_out, index * chunk, chunk, axis=1)
 
     def gradients(now):
-        parts = [backward(info, now, grad_heads, kv_all, att_t, lse, span, g) for g in range(kvl)]
-        queries_part = jnp.concatenate([part[0] for part in parts], axis=1)
-        terms = jnp.stack([part[1] for part in parts], axis=1).reshape(ctx, kvl, 2, rows, hd)
+        queries_part, terms = backward(info, now, grad_heads, kv_all, att_t, lse, span)
+        terms = terms.reshape(ctx, kvl, 2, rows, hd)
         return queries_part, lax.psum_scatter(terms, "ctx", scatter_dimension=0, tiled=False)
 
     grads = None

time: 174 us -> 172 us (0.989)
    pallas_call x2 -> x1, Pallas kernels: 22.1 us -> 21.5 us  [backward(): pl.pallas_call(kernel, out_shape=(jax.ShapeDtypeStruct((rows, flat), BF16...]
  transfers between devices with their start and end apart: 8 -> 8, of which waited for: 5 -> 5; matrix products, arithmetic and copies ran while one was open for 17% -> 16% of each run, Pallas kernels for 23% -> 23%
where the time goes in v4:
time: 172 us; the launch traced here: 171 us
  Pallas kernels  58.6 us (34%)
  waiting for transfers between devices  42.8 us (25%)
  starting transfers between devices  18.9 us (11%)
  matrix products  16.9 us (10%)
  between operations  14.1 us (8%)
  other arithmetic  12.8 us (7%)
  local copies, waits for them, and re-layouts  7.27 us (4%)
    pallas_call x2, Pallas kernels, project(): pl.pallas_call(project_kernel, out_shape=jax.ShapeDtypeStruct((rows, widt...  22 us
    pallas_call x1, Pallas kernels, backward(): pl.pallas_call(kernel, out_shape=(jax.ShapeDtypeStruct((rows, flat), BF16...  21.5 us
    ppermute x3, waiting for transfers between devices, local(): from_right = lax.ppermute(left, 'tp', to_left).astype(F32)  19.2 us
    dot_general x1, matrix products, local(): lax.dot_general(grad_out, out_weight, (((1,), (1,)), ((), ())), preferred...  16.9 us
    pallas_call x1, Pallas kernels, forward(): pl.pallas_call(kernel, out_shape=(jax.ShapeDtypeStruct((rows, flat), BF16...  15.1 us
    ppermute x3, starting transfers between devices, local(): from_left = lax.ppermute(right, 'tp', to_right).astype(F32)  14.2 us
    all_gather x1, waiting for transfers between devices, local(): kv_all = lax.all_gather(kv, 'ctx', axis=0, tiled=False)  12.9 us
    convert_element_type x2, other arithmetic, local(): left = (own_part(k + 2 - tp + me).astype(F32) + from_right).astype(BF16)  8.47 us
  transfers between devices with their start and end apart: 8, of which 5 were waited for; matrix products, arithmetic and copies ran while one was open for 16% of the time, Pallas kernels for 23%

profile of v4, /device:TPU:0, one launch (start us, length us, event | category | flops | bytes accessed | tf_op | source)
XLA Modules:
  0.0 171.3 jit_solution(6485982968022557168)
XLA Ops:
  7.2 1.4 maximum_bitcast_fusion
  9.4 1.5 copy.25
  10.9 16.9 %convolution_convert_fusion.go_ref = bf16[256,2048]{1,0:T(8,128)(2,1)} fusion(bf16[256,8192]{1,0:T(8,128)(2,1)} %param.11, bf16[2048,8192]{1,0:T(8,128)(2,1)} %w_ref.3), kind=kOutput, calls=%fused_computation | convolution fusion | flops 8590458880 | bytes 38797312 | tf_op jit(solution)/shard_map/dot_general | solution.py:329
  28.2 12.9 %all-gather.2.cloned.1.call-done.k_ref.v_ref = bf16[8,4,2,128,128]{4,3,2,1,0:T(8,128)(2,1)} async-done(((bf16[1,4,2,128,128]{4,3,2,1,0:T(8,128)(2,1)}), bf16[8,4,2,128,128]{4,3,2,1,0:T(8,128)(2,1)}) %all-gather.2.cloned.1.call-update) | async-done | bytes 2097168 | tf_op jit(solution)/shard_map/all_gather | solution.py:320
  41.1 15.1 %shard_map.93 = (bf16[256,2048]{1,0:T(8,128)(2,1)S(1)}, bf16[2,2,128,1024]{3,2,1,0:T(8,128)(2,1)S(1)}, f32[2,2,1,1024]{3,2,1,0:T(1,128)S(1)}) custom-call(s32[18]{0:T(128)S(1)} %pad_add_fusion.info_ref, bf16[256,2048]{1,0:T(8,128)(2,1)S(1)} %bitcast.23, bf16[8,4,2,128,128]{4,3,2,1,0:T(8,128)(2,1)} %all-gather.2.cloned.1.call-done.k_ref.v_ref, ...), custom_call_target="tpu_custom_call" | custom-call | flops 4294967296 | bytes 2097152 | tf_op jit(solution)/shard_map/pallas_call | solution.py:218
  56.2 1.1 copy-done
  57.3 4.8 %shard_map.94 = bf16[256,2048]{1,0:T(8,128)(2,1)S(1)} custom-call(s32[1]{0:T(128)} %bitcast.info_ref, bf16[256,2048]{1,0:T(8,128)(2,1)S(1)} %get-tuple-element.20.a_ref, bf16[2048,8192]{1,0:T(8,128)(2,1)} %w_ref.3), custom_call_target="tpu_custom_call" | custom-call | flops 2147483648 | bytes 8388608 | tf_op jit(solution)/shard_map/pallas_call | solution.py:190
  62.1 1.7 collective-permute-start.1
  63.7 4.4 %collective-permute-start = (bf16[256,2048]{1,0:T(8,128)(2,1)S(1)}, bf16[256,2048]{1,0:T(8,128)(2,1)}, u32[]{:S(2)}, u32[]{:S(2)}) collective-permute-start(bf16[256,2048]{1,0:T(8,128)(2,1)S(1)} %shard_map.94), channel_id=1, source_target_pairs={{0,1},{4,5},{8,9},{12,13},{16,17},{20,21},{24,25},{28,29}} | collective-permute-start | bytes 3145736 | tf_op jit(solution)/shard_map/ppermute | solution.py:355
  68.1 17.3 %shard_map.95 = bf16[256,8192]{1,0:T(8,128)(2,1)} custom-call(s32[1]{0:T(128)} %constant.15.clone.1.info_ref, bf16[256,2048]{1,0:T(8,128)(2,1)S(1)} %get-tuple-element.20.a_ref, bf16[2048,8192]{1,0:T(8,128)(2,1)} %w_ref.3), custom_call_target="tpu_custom_call" | custom-call | flops 8589934592 | bytes 33554432 | tf_op jit(solution)/shard_map/pallas_call | solution.py:190
  85.4 4.6 %collective-permute-done = bf16[256,2048]{1,0:T(8,128)(2,1)} collective-permute-done((bf16[256,2048]{1,0:T(8,128)(2,1)S(1)}, bf16[256,2048]{1,0:T(8,128)(2,1)}, u32[]{:S(2)}, u32[]{:S(2)}) %collective-permute-start) | collective-permute-done | bytes 1048608 | tf_op jit(solution)/shard_map/ppermute | solution.py:355
  90.0 4.0 %add_convert_fusion.3 = (bf16[256,2048]{1,0:T(8,128)(2,1)}, bf16[256,2048]{1,0:T(8,128)(2,1)S(1)}) fusion(bf16[256,2048]{1,0:T(8,128)(2,1)} %collective-permute-done.1, bf16[256,8192]{1,0:T(8,128)(2,1)} %shard_map.95, s32[]{:T(128)S(6)} %select_n.42, bf16[256,2048]{1,0:T(8,128)(2,1)} %collective-permute-done, s32[]{:T(128)S(6)} %select_n.41), kind=kLoop, calls=%fused_computation.4 | loop fusion | flops 4194304 | bytes 6291464 | tf_op jit(solution)/shard_map/convert_element_type | solution.py:359
  93.9 1.6 collective-permute-start.3
  95.5 5.2 %collective-permute-start.2 = (bf16[256,2048]{1,0:T(8,128)(2,1)S(1)}, bf16[256,2048]{1,0:T(8,128)(2,1)}, u32[]{:S(2)}, u32[]{:S(2)}) collective-permute-start(bf16[256,2048]{1,0:T(8,128)(2,1)S(1)} %get-tuple-element.22), channel_id=1, source_target_pairs={{0,1},{1,2},{4,5},{5,6},{8,9},{9,10},{12,13},{13,14},{16,17},{17,1... | collective-permute-start | bytes 3145736 | tf_op jit(solution)/shard_map/ppermute | solution.py:355
  100.7 21.5 %shard_map.96 = (bf16[256,2048]{1,0:T(8,128)(2,1)S(1)}, bf16[8,2,2,2,128,128]{5,4,3,2,1,0:T(8,128)(2,1)}) custom-call(s32[18]{0:T(128)S(1)} %pad_add_fusion.info_ref, bf16[256,2048]{1,0:T(8,128)(2,1)S(1)} %bitcast.24, bf16[256,2048]{1,0:T(8,128)(2,1)S(1)} %copy-done.1, bf16[8,4,2,128,128]{4,3,2,1,0:T(8,128)(2,1)} %all-gather.2.cloned.1.call-done.k_ref.v_ref, ...), custom_call_target="tpu_custom_call" | custom-call | flops 10737418240 | bytes 2097152 | tf_op jit(solution)/shard_map/pallas_call | solution.py:265
  122.3 4.5 %add_convert_fusion.1 = (bf16[256,2048]{1,0:T(8,128)(2,1)}, bf16[256,2048]{1,0:T(8,128)(2,1)}) fusion(bf16[256,2048]{1,0:T(8,128)(2,1)} %collective-permute-done.3, bf16[256,8192]{1,0:T(8,128)(2,1)} %shard_map.95, s32[]{:T(128)S(6)} %select_n.43, bf16[256,2048]{1,0:T(8,128)(2,1)} %collective-permute-done.2, s32[]{:T(128)S(6)} %select_n.40), kind=kLoop, calls=%fused_computation.2 | loop fusion | flops 4194304 | bytes 6291464 | tf_op jit(solution)/shard_map/convert_element_type | solution.py:359
  126.7 1.3 collective-permute-start.5
  128.0 4.7 %collective-permute-start.4 = (bf16[256,2048]{1,0:T(8,128)(2,1)}, bf16[256,2048]{1,0:T(8,128)(2,1)S(1)}, u32[]{:S(2)}, u32[]{:S(2)}) collective-permute-start(bf16[256,2048]{1,0:T(8,128)(2,1)} %get-tuple-element.25), channel_id=1, source_target_pairs={{0,1},{1,2},{2,3},{4,5},{5,6},{6,7},{8,9},{9,10},{10,11},{12,13},{... | collective-permute-start | bytes 3145736 | tf_op jit(solution)/shard_map/ppermute | solution.py:355
  132.7 1.2 copy.23
  133.9 19.2 %collective-permute-done.5 = bf16[256,2048]{1,0:T(8,128)(2,1)S(1)} collective-permute-done((bf16[256,2048]{1,0:T(8,128)(2,1)}, bf16[256,2048]{1,0:T(8,128)(2,1)S(1)}, u32[]{:S(2)}, u32[]{:S(2)}) %collective-permute-start.5) | collective-permute-done | bytes 1048608 | tf_op jit(solution)/shard_map/ppermute | solution.py:356
  153.1 1.3 collective-permute-done.4
  154.4 2.7 %add_convert_fusion = bf16[256,2048]{1,0:T(8,128)(2,1)} fusion(bf16[256,2048]{1,0:T(8,128)(2,1)S(1)} %collective-permute-done.5, bf16[256,2048]{1,0:T(8,128)(2,1)S(1)} %collective-permute-done.4, bf16[256,8192]{1,0:T(8,128)(2,1)} %shard_map.95, s32[]{:T(128)S(6)} %select_n.39), kind=kLoop, calls=%fused_computation.1 | loop fusion | flops 3145728 | bytes 4194308 | tf_op jit(solution)/shard_map/convert_element_type | solution.py:365
  157.1 4.8 %reduce-scatter.2.cloned.1.call-done = bf16[1,2,2,256,128]{4,3,2,1,0:T(8,128)(2,1)} async-done(((bf16[8,2,2,256,128]{4,3,2,1,0:T(8,128)(2,1)}), bf16[1,2,2,256,128]{4,3,2,1,0:T(8,128)(2,1)}) %reduce-scatter.2.cloned.1.call-update) | async-done | bytes 262160 | tf_op jit(solution)/shard_map/reduce_scatter | solution.py:348
  161.9 1.0 slice_bitcast_fusion
  (20 shorter events, 2.9 us)
Async XLA Ops:
  7.2 33.9 %all-gather.2.cloned.1.call-start = ((), (), s32[]{:S(2)}) async-start(), calls=%async_computation.1 | async-start | bytes 2359296 | tf_op jit(solution)/shard_map/all_gather | solution.py:320
  9.3 152.6 %reduce-scatter.2.cloned.1.call-start = ((), (), s32[]{:S(2)}) async-start(), calls=%async_computation.2 | async-start | bytes 2359296 | tf_op jit(solution)/shard_map/reduce_scatter | solution.py:348
  10.9 16.9 %copy-start.2 = (s32[2048]{0:T(1024)S(1)}, s32[2048]{0:T(1024)}, u32[]{:S(2)}) copy-start(s32[2048]{0:T(1024)} %param.9) | copy-start | bytes 24580
  56.2 1.1 copy-start
  62.1 23.3 %collective-permute-start.1 = (bf16[256,2048]{1,0:T(8,128)(2,1)S(1)}, bf16[256,2048]{1,0:T(8,128)(2,1)}, u32[]{:S(2)}, u32[]{:S(2)}) collective-permute-start(bf16[256,2048]{1,0:T(8,128)(2,1)S(1)} %shard_map.94), channel_id=1, source_target_pairs={{3,2},{7,6},{11,10},{15,14},{19,18},{23,22},{27,26},{31,30}} | collective-permute-start | bytes 3145736 | tf_op jit(solution)/shard_map/ppermute | solution.py:356
  63.7 26.2 %collective-permute-start = (bf16[256,2048]{1,0:T(8,128)(2,1)S(1)}, bf16[256,2048]{1,0:T(8,128)(2,1)}, u32[]{:S(2)}, u32[]{:S(2)}) collective-permute-start(bf16[256,2048]{1,0:T(8,128)(2,1)S(1)} %shard_map.94), channel_id=1, source_target_pairs={{0,1},{4,5},{8,9},{12,13},{16,17},{20,21},{24,25},{28,29}} | collective-permute-start | bytes 3145736 | tf_op jit(solution)/shard_map/ppermute | solution.py:355
  85.4 15.3 %copy-start.1 = (bf16[256,2048]{1,0:T(8,128)(2,1)S(1)}, bf16[256,2048]{1,0:T(8,128)(2,1)}, u32[]{:S(2)}) copy-start(bf16[256,2048]{1,0:T(8,128)(2,1)} %convolution_convert_fusion.go_ref) | copy-start | bytes 3145732
  93.9 28.3 %collective-permute-start.3 = (bf16[256,2048]{1,0:T(8,128)(2,1)}, bf16[256,2048]{1,0:T(8,128)(2,1)}, u32[]{:S(2)}, u32[]{:S(2)}) collective-permute-start(bf16[256,2048]{1,0:T(8,128)(2,1)} %get-tuple-element.23), channel_id=1, source_target_pairs={{3,2},{2,1},{7,6},{6,5},{11,10},{10,9},{15,14},{14,13},{19,18},{18... | collective-permute-start | bytes 3145736 | tf_op jit(solution)/shard_map/ppermute | solution.py:356
  95.5 26.7 %collective-permute-start.2 = (bf16[256,2048]{1,0:T(8,128)(2,1)S(1)}, bf16[256,2048]{1,0:T(8,128)(2,1)}, u32[]{:S(2)}, u32[]{:S(2)}) collective-permute-start(bf16[256,2048]{1,0:T(8,128)(2,1)S(1)} %get-tuple-element.22), channel_id=1, source_target_pairs={{0,1},{1,2},{4,5},{5,6},{8,9},{9,10},{12,13},{13,14},{16,17},{17,1... | collective-permute-start | bytes 3145736 | tf_op jit(solution)/shard_map/ppermute | solution.py:355
  126.7 26.3 %collective-permute-start.5 = (bf16[256,2048]{1,0:T(8,128)(2,1)}, bf16[256,2048]{1,0:T(8,128)(2,1)S(1)}, u32[]{:S(2)}, u32[]{:S(2)}) collective-permute-start(bf16[256,2048]{1,0:T(8,128)(2,1)} %get-tuple-element.26), channel_id=1, source_target_pairs={{3,2},{2,1},{1,0},{7,6},{6,5},{5,4},{11,10},{10,9},{9,8},{15,14},{... | collective-permute-start | bytes 3145736 | tf_op jit(solution)/shard_map/ppermute | solution.py:356
  128.0 26.3 %collective-permute-start.4 = (bf16[256,2048]{1,0:T(8,128)(2,1)}, bf16[256,2048]{1,0:T(8,128)(2,1)S(1)}, u32[]{:S(2)}, u32[]{:S(2)}) collective-permute-start(bf16[256,2048]{1,0:T(8,128)(2,1)} %get-tuple-element.25), channel_id=1, source_target_pairs={{0,1},{1,2},{2,3},{4,5},{5,6},{6,7},{8,9},{9,10},{10,11},{12,13},{... | collective-permute-start | bytes 3145736 | tf_op jit(solution)/shard_map/ppermute | solution.py:355
Sparse Core Ops, SparseCore 0:
  10.5 30.5 all-gather.1
  122.3 39.5 reduce-scatter.1
